TPU v7x, 512 devices: a whole 4x8x8 slice. The times are simulated.
512 devices in a mesh: var: 128 (over z, y, core), dp: 4 (over x).
Axes of the slice: x: 4, y: 8, z: 8, core: 2. Of those that a mesh axis runs over, the one named last changes fastest.
Arguments:
- fields: bfloat16 [4, 128, 256, 16], P('dp', 'var')
- presence: int32 [4, 128], P('dp'), may hold values from 0 to 1, as said below
- slot_var: int32 [128], replicated, may hold values from 0 to 127, each once
- patch_weight: bfloat16 [128, 16, 1024], P('var'), may hold values from -1.5 to 1.5
- var_embed: bfloat16 [128, 1024], P('var'), may hold values from -3 to 3
- query: float32 [1024], replicated
- key_weight: bfloat16 [1024, 1024], replicated, may hold values from -0.1875 to 0.1875
- value_weight: bfloat16 [1024, 1024], replicated, may hold values from -0.1875 to 0.1875
- out_grad: bfloat16 [4, 256, 1024], P('dp', 'var'), may hold values from -6 to 6
Outputs:
- mixed: bfloat16 [4, 256, 1024], P('dp', 'var')
- grad_patch_weight: float32 [128, 16, 1024], P('var')
- grad_var_embed: float32 [128, 1024], P('var')
- grad_query: float32 [1024], replicated
Inputs may be any that keep to these rules, and one draw needn't show every extreme that they name: `presence`: every sample has at least one present variable.
All inputs are finite; a program needn't handle non-finite values.
Results may differ from a plain program's by a relative error of at most 0.0065.
The roundings to bfloat16 on the way count: a program that leaves them out, or rounds other values in their place, can miss the bound.
Values may be sent and summed in bfloat16 or wider, within the bound.
No kernel may reach another device: no remote copies, remote signals or barrier semaphores. Data moves between devices by JAX's collectives and lax.ppermute only.
A program may use at most 64 MiB of HBM per device.

v0:
```python
import math

import jax
import jax.numpy as jnp
from jax import lax
from jax.sharding import PartitionSpec as P

HEADS = 16


field_eps = 1e-05
key_eps = 1e-06
masked_low = -1e30
highest = lax.Precision.HIGHEST


def slot_presence(presence, slot_var):
    lookup = (slot_var[:, None] == jnp.arange(presence.shape[1], dtype=jnp.int32)[None, :]).astype(
        jnp.int32
    )
    return jnp.sum(presence[:, None, :] * lookup[None, :, :], axis=2)


def masked_softmax(scores, valid_mask):
    row_max = jnp.max(jnp.where(valid_mask, scores, masked_low), axis=-1, keepdims=True)
    weights = jnp.where(valid_mask, jnp.exp(scores - row_max), 0.0)
    return weights / jnp.sum(weights, axis=-1, keepdims=True)


def key_heads(tokens, key_weight, head_count):
    model_width = key_weight.shape[0]
    raw_keys = jnp.dot(
        tokens.reshape(-1, model_width), key_weight, preferred_element_type=jnp.float32
    )
    raw_keys = raw_keys.reshape(tokens.shape[:-1] + (head_count, model_width // head_count))
    key_ratio = lax.rsqrt(jnp.mean(raw_keys * raw_keys, axis=-1) + key_eps)
    return (raw_keys * key_ratio[..., None], key_ratio)


def token_grads(
    dscore,
    attention,
    grad_heads,
    normed_keys,
    key_ratio,
    query_heads,
    score_scale,
    key_weight,
    value_weight,
):
    norm_grad = dscore[..., None] * query_heads * score_scale
    key_grad = key_ratio[..., None] * (
        norm_grad - normed_keys * jnp.mean(norm_grad * normed_keys, axis=-1, keepdims=True)
    )
    value_grad = attention[..., None] * grad_heads
    model_width = key_weight.shape[0]
    lead_dims = key_grad.shape[:-2]
    contract = (((1,), (1,)), ((), ()))
    token_total = lax.dot_general(
        key_grad.astype(jnp.bfloat16).reshape(-1, model_width),
        key_weight,
        contract,
        preferred_element_type=jnp.float32,
    )
    token_total = token_total + lax.dot_general(
        value_grad.astype(jnp.bfloat16).reshape(-1, model_width),
        value_weight,
        contract,
        preferred_element_type=jnp.float32,
    )
    return token_total.astype(jnp.bfloat16).reshape(lead_dims + (model_width,))


def on_device(
    fields, presence, slot_var, patch_weight, var_embed, query, key_weight, value_weight, out_grad
):
    var_count = lax.axis_size("var")
    own_index = lax.axis_index("var")
    batch_size, own_vars, patches, pixels = fields.shape
    model_width = key_weight.shape[0]
    head_dim = model_width // HEADS
    score_scale = 1.0 / math.sqrt(head_dim)
    local_patches = patches // var_count
    query_heads = query.reshape(HEADS, head_dim)
    slot_flags = slot_presence(presence, slot_var)
    all_valid = (slot_flags > 0)[:, None, None, :]
    own_flags = lax.dynamic_slice_in_dim(slot_flags, own_index * own_vars, own_vars, 1).astype(
        jnp.float32
    )
    values = fields.astype(jnp.float32)
    weighted = own_flags[:, :, None, None] * values
    cell_count = patches * pixels
    first_sum, present = lax.psum(
        (jnp.sum(weighted, axis=(0, 2, 3)), jnp.sum(own_flags, axis=0)), "dp"
    )
    cell_total = jnp.maximum(present, 1.0) * cell_count
    mean_value = first_sum / cell_total
    centered = values - mean_value[None, :, None, None]
    second_sum = lax.psum(
        jnp.sum(own_flags[:, :, None, None] * centered * centered, axis=(0, 2, 3)), "dp"
    )
    spread = second_sum / cell_total
    normed = (centered * lax.rsqrt(spread + field_eps)[None, :, None, None]).astype(jnp.bfloat16)
    tokens = jnp.einsum("bvpe,ved->bvpd", normed, patch_weight, preferred_element_type=jnp.float32)
    tokens = (tokens + var_embed.astype(jnp.float32)[None, :, None, :]).astype(jnp.bfloat16)
    gathered = lax.all_to_all(tokens, "var", split_axis=2, concat_axis=1, tiled=True)
    grad_local = out_grad.astype(jnp.float32).reshape(batch_size, local_patches, HEADS, head_dim)
    normed_keys, key_ratio = key_heads(gathered, key_weight, HEADS)
    scores = jnp.einsum("bsphe,he->bphs", normed_keys, query_heads, precision=highest) * score_scale
    attention = masked_softmax(scores, all_valid)
    value_rows = jnp.dot(
        gathered.reshape(-1, model_width), value_weight, preferred_element_type=jnp.float32
    )
    value_rows = value_rows.reshape(gathered.shape[:-1] + (HEADS, head_dim))
    heads_out = jnp.einsum("bphs,bsphe->bphe", attention, value_rows, precision=highest)
    attn_grad = jnp.einsum("bphe,bsphe->bphs", grad_local, value_rows, precision=highest)
    dscore = attention * (attn_grad - jnp.sum(attention * attn_grad, axis=-1, keepdims=True))
    dquery = jnp.einsum("bphs,bsphe->he", dscore, normed_keys, precision=highest) * score_scale
    outgoing = token_grads(
        jnp.transpose(dscore, (0, 3, 1, 2)),
        jnp.transpose(attention, (0, 3, 1, 2)),
        grad_local[:, None],
        normed_keys,
        key_ratio,
        query_heads,
        score_scale,
        key_weight,
        value_weight,
    )
    returned = lax.all_to_all(outgoing, "var", split_axis=1, concat_axis=2, tiled=True)
    mixed_out = heads_out.reshape(batch_size, local_patches, model_width).astype(jnp.bfloat16)
    dweight = jnp.einsum("bvpe,bvpd->ved", normed, returned, preferred_element_type=jnp.float32)
    dembed = jnp.sum(returned.astype(jnp.float32), axis=(0, 2))
    dweight, dembed = lax.psum((dweight, dembed), "dp")
    dquery = lax.psum(dquery.reshape(model_width), ("var", "dp"))
    return (mixed_out, dweight, dembed, dquery)


def solution(mesh):
    return jax.shard_map(
        on_device,
        mesh=mesh,
        in_specs=(
            P("dp", "var", None, None),
            P("dp", None),
            P(),
            P("var", None, None),
            P("var", None),
            P(),
            P(),
            P(),
            P("dp", "var", None),
        ),
        out_specs=(P("dp", "var", None), P("var", None, None), P("var", None), P()),
        check_vma=False,
    )
```

profile of v0, /device:TPU:1, one launch (start us, length us, event | category | flops | bytes accessed | tf_op | source)
XLA Modules:
  0.0 306.9 jit_solution(3596393881065953439)
XLA Ops:
  7.2 0.8 add.55
  8.0 0.8 select_reduce_fusion
  8.9 0.6 dynamic-slice.3
  10.1 1.3 fusion.23
  11.4 10.4 %all-reduce = (f32[1]{0:T(128)}, f32[1]{0:T(128)}) all-reduce(f32[1]{0:T(128)} %bitcast.5, f32[1]{0:T(128)} %convert_element_type.59), channel_id=1, replica_groups=mesh['var'=128,'dp'=4] {'dp'}, use_global_device_ids=true, to_apply=%region_2.0 | all-reduce | flops 2 | bytes 16 | tf_op jit(solution)/shard_map/psum | solution.py:93
  23.2 1.3 fusion.24
  24.5 6.6 %psum.44 = f32[1]{0:T(128)} all-reduce(f32[1]{0:T(128)} %bitcast.7), channel_id=1, replica_groups=mesh['var'=128,'dp'=4] {'dp'}, use_global_device_ids=true, to_apply=%region_5.0 | all-reduce | flops 1 | bytes 8 | tf_op jit(solution)/shard_map/psum | solution.py:99
  31.8 1.1 fusion.3
  32.9 0.8 copy.57
  33.7 0.5 broadcast.167
  34.2 4.5 %reduce.15 = bf16[256,1024]{1,0:T(8,128)(2,1)} reduce(bf16[256,1,1,1024]{3,2,1,0:T(2,128)(2,1)S(1)} %bitcast.137, bf16[]{:T(256)} %broadcast.167), dimensions={1,2}, to_apply=%bitcast.134.reduce_sub_computation | reduce | bytes 1048578
  38.7 2.0 reshape.316
  40.8 21.8 %all-to-all-start = ((bf16[128,2,1024]{2,1,0:T(2,128)(2,1)}), bf16[128,2,1024]{2,1,0:T(2,128)(2,1)}, u32[]{:S(2)}, u32[]{:S(2)}) async-start(bf16[128,2,1024]{2,1,0:T(2,128)(2,1)} %reshape.316), calls=%async_computation | async-start | bytes 1048576 | tf_op jit(solution)/shard_map/all_to_all | solution.py:106
  62.6 0.1 reshape.314
  62.7 0.1 reshape.297
  62.8 4.0 %copy.25 = bf16[1024,1024]{0,1:T(8,128)(2,1)} copy(bf16[1024,1024]{1,0:T(8,128)(2,1)} %param.16) | data formatting | bytes 4194304 | tf_op args[7]
  66.8 0.1 reshape.295
  66.8 0.6 mul.265
  67.4 15.4 %all-to-all-done = bf16[128,2,1024]{2,1,0:T(2,128)(2,1)} async-done(((bf16[128,2,1024]{2,1,0:T(2,128)(2,1)}), bf16[128,2,1024]{2,1,0:T(2,128)(2,1)}, u32[]{:S(2)}, u32[]{:S(2)}) %all-to-all-start) | async-done | bytes 524320 | tf_op jit(solution)/shard_map/all_to_all | solution.py:106
  82.8 3.6 %reshape.317 = bf16[256,1,1,1024]{3,2,1,0:T(2,128)(2,1)S(1)} reshape(bf16[128,2,1024]{2,1,0:T(2,128)(2,1)} %all-to-all-done) | data formatting | bytes 1048576
  86.4 3.8 %bitcast_reduce_fusion = bf16[256,1024]{1,0:T(8,128)(2,1)} fusion(bf16[256,1,1,1024]{3,2,1,0:T(2,128)(2,1)S(1)} %reshape.317), kind=kLoop, calls=%fused_computation.58 | loop fusion | bytes 1048576 | tf_op jit(solution)/shard_map/all_to_all | solution.py:106
  90.2 1.9 fusion.5
  92.2 1.9 reshape.293
  94.1 1.8 reshape.294
  95.9 2.1 dot_general.49
  98.0 2.5 fusion.8
  100.5 1.0 copy-done.2
  101.5 0.6 fusion.34
  102.1 0.1 copy.38
  102.3 2.4 multiply_reduce_fusion.3
  104.7 0.1 add_rsqrt_fusion
  104.8 1.4 multiply_reduce_fusion.1
  106.2 0.2 fusion.17
  106.4 0.2 fusion.26
  106.6 0.8 fusion.15
  107.5 0.2 fusion.16
  107.7 0.9 fusion.29
  108.6 1.0 copy.35
  109.6 2.0 mul.233
  111.5 2.8 mul.239
  114.3 6.0 %multiply_reduce_fusion.2 = f32[128,2,16]{2,1,0:T(2,128)S(1)} fusion(f32[1,128,2,16,64]{4,3,2,1,0:T(8,128)} %reshape.294, f32[128,2,16]{2,1,0:T(2,128)S(1)} %add_rsqrt_fusion, f32[16,64]{1,0:T(8,128)S(1)} %reshape.295, f32[128,2,16]{2,1,0:T(2,128)S(1)} %get-tuple-element.7), kind=kLoop, calls=%fused_computation.3 | loop fusion | flops 1306624 | bytes 1101824 | tf_op jit(solution)/shard_map/reduce_sum | solution.py:53
  120.3 0.1 broadcast_multiply_fusion
  120.3 1.9 mul.258
  122.2 2.8 mul.259
  125.0 1.9 mul.243
  126.9 2.8 mul.244
  129.7 1.6 multiply_convert_fusion
  131.3 2.6 convert_element_type.67
  133.9 2.8 fusion.4
  136.7 1.5 fusion.2
  138.3 2.1 reshape.298
  140.4 6.4 %all-to-all-start.1 = ((bf16[1,128,2,1024]{3,2,0,1:T(2,128)(2,1)}), bf16[1,128,2,1024]{3,2,0,1:T(2,128)(2,1)}, u32[]{:S(2)}, u32[]{:S(2)}) async-start(bf16[1,128,2,1024]{3,2,0,1:T(2,128)(2,1)} %bitcast.139), calls=%async_computation.1 | async-start | bytes 1048576 | tf_op jit(solution)/shard_map/all_to_all | solution.py:130
  146.9 0.0 all-reduce.3.cloned.1.call-start
  146.9 1.7 fusion.33
  148.7 0.7 convert_element_type.64
  149.4 3.1 %multiply_reduce_fusion = f32[16,64]{1,0:T(8,128)S(1)} fusion(f32[128,2,16,64]{3,2,1,0:T(8,128)} %reshape.293, f32[16,2,128]{0,1,2:T(2,128)S(1)} %copy-done.8, f32[128,2,16]{2,1,0:T(2,128)S(1)} %add_rsqrt_fusion), kind=kLoop, calls=%fused_computation | loop fusion | flops 785408 | bytes 1085440 | tf_op jit(solution)/shard_map/bphs,bsphe->he/dot_general | solution.py:118
  152.5 0.1 reshape.301
  152.6 98.2 %psum.47 = f32[1024]{0:T(1024)} all-reduce(f32[1024]{0:T(1024)S(1)} %reshape.301), channel_id=1, replica_groups=mesh['var'=128,'dp'=4] {'var','dp'}, use_global_device_ids=true, to_apply=%region_14.15 | all-reduce | flops 1024 | bytes 8192 | tf_op jit(solution)/shard_map/psum | solution.py:135
  250.7 1.2 reshape.299
  252.0 0.8 convolution_bitcast_fusion.1
  252.8 1.5 convert_reduce_fusion
  254.4 7.6 %psum.46 = f32[1,1024]{1,0:T(1,128)} all-reduce(f32[1,1024]{1,0:T(1,128)S(1)} %bitcast.142), channel_id=1, replica_groups=mesh['var'=128,'dp'=4] {'dp'}, use_global_device_ids=true, to_apply=%region_13.14 | all-reduce | flops 1024 | bytes 8192 | tf_op jit(solution)/shard_map/psum | solution.py:134
  261.9 36.6 %all-reduce.3.cloned.1.call-done = f32[1,16,1024]{2,1,0:T(8,128)} async-done(((f32[1,16,1024]{2,1,0:T(8,128)}), f32[1,16,1024]{2,1,0:T(8,128)}) %all-reduce.3.cloned.1.call-update) | async-done | bytes 65552 | tf_op jit(solution)/shard_map/psum | solution.py:134
  298.6 1.5 copy.60
  (30 shorter events, 0.1 us)
Async XLA Ops:
  7.2 83.1 %copy-start = (bf16[1024,1024]{1,0:T(8,128)(2,1)S(1)}, bf16[1024,1024]{1,0:T(8,128)(2,1)}, u32[]{:S(2)}) copy-start(bf16[1024,1024]{1,0:T(8,128)(2,1)} %param.15) | copy-start | bytes 6291460
  33.7 28.9 %copy-start.12 = (bf16[1,2,1024]{2,1,0:T(2,128)(2,1)S(1)}, bf16[1,2,1024]{2,1,0:T(2,128)(2,1)}, u32[]{:S(2)}) copy-start(bf16[1,2,1024]{2,1,0:T(2,128)(2,1)} %param.17) | copy-start | bytes 12292
  40.8 42.0 %all-to-all-start = ((bf16[128,2,1024]{2,1,0:T(2,128)(2,1)}), bf16[128,2,1024]{2,1,0:T(2,128)(2,1)}, u32[]{:S(2)}, u32[]{:S(2)}) async-start(bf16[128,2,1024]{2,1,0:T(2,128)(2,1)} %reshape.316), calls=%async_computation | async-start | bytes 1048576 | tf_op jit(solution)/shard_map/all_to_all | solution.py:106
  62.8 4.0 %copy-start.11 = (f32[1024]{0:T(1024)S(1)}, f32[1024]{0:T(1024)}, u32[]{:S(2)}) copy-start(f32[1024]{0:T(1024)} %param.14) | copy-start | bytes 12292
  86.4 3.8 %copy-start.5 = (bf16[256,1,1,1024]{3,2,1,0:T(2,128)(2,1)}, bf16[256,1,1,1024]{3,2,1,0:T(2,128)(2,1)S(1)}, u32[]{:S(2)}) copy-start(bf16[256,1,1,1024]{3,2,1,0:T(2,128)(2,1)S(1)} %reshape.317) | copy-start | bytes 1572868
  100.5 1.0 copy-start.2
  102.2 2.5 copy-start.1
  126.9 2.8 copy-start.7
  126.9 2.8 copy-start.10
  133.9 2.8 copy-start.4
  133.9 2.8 copy-start.6
  138.3 8.6 %copy-start.3 = (f32[128,2,16,64]{0,3,2,1:T(8,128)S(1)}, f32[128,2,16,64]{0,3,2,1:T(8,128)}, u32[]{:S(2)}) copy-start(f32[128,2,16,64]{0,3,2,1:T(8,128)} %copy-done.2) | copy-start | bytes 3145732
  138.3 11.1 %copy-start.8 = (f32[16,2,128]{0,1,2:T(2,128)S(1)}, f32[16,2,128]{0,1,2:T(2,128)}, u32[]{:S(2)}) copy-start(f32[16,2,128]{0,1,2:T(2,128)} %get-tuple-element.6) | copy-start | bytes 49156
  140.4 110.3 %all-to-all-start.1 = ((bf16[1,128,2,1024]{3,2,0,1:T(2,128)(2,1)}), bf16[1,128,2,1024]{3,2,0,1:T(2,128)(2,1)}, u32[]{:S(2)}, u32[]{:S(2)}) async-start(bf16[1,128,2,1024]{3,2,0,1:T(2,128)(2,1)} %bitcast.139), calls=%async_computation.1 | async-start | bytes 1048576 | tf_op jit(solution)/shard_map/all_to_all | solution.py:130
  146.9 105.1 %copy-start.9 = (bf16[1,1,256,16]{2,3,1,0:T(8,128)(2,1)S(1)}, bf16[1,1,256,16]{2,3,1,0:T(8,128)(2,1)}, u32[]{:S(2)}) copy-start(bf16[1,1,256,16]{2,3,1,0:T(8,128)(2,1)} %param.9) | copy-start | bytes 24580
  146.9 151.7 %all-reduce.3.cloned.1.call-start = ((), (), s32[]{:S(2)}) async-start(), calls=%async_computation.2 | async-start | bytes 131072 | tf_op jit(solution)/shard_map/psum | solution.py:134
Sparse Core Ops, SparseCore 0:
  253.0 45.5 all-reduce.2
where the time goes:
time: 309 us; the launch traced here: 307 us
  blocking collectives  123 us (40%)
  waiting for transfers between devices  52 us (17%)
  local copies, waits for them, and re-layouts  45.8 us (15%)
  starting transfers between devices  28.3 us (9%)
  other arithmetic  28 us (9%)
  between operations  17 us (6%)
  matrix products  13.1 us (4%)
    psum x1, blocking collectives, on_device(): dquery = lax.psum(dquery.reshape(model_width), ('var', 'dp'))  98.2 us
    psum x1, waiting for transfers between devices, on_device(): dweight, dembed = lax.psum((dweight, dembed), 'dp')  36.6 us
    all_to_all x1, starting transfers between devices, on_device(): lax.all_to_all(tokens, 'var', split_axis=2, concat_axis=1, tiled=True)  21.8 us
    all_to_all x1, waiting for transfers between devices, on_device(): lax.all_to_all(tokens, 'var', split_axis=2, concat_axis=1, tiled=True)  15.4 us
    unnamed x31, local copies, waits for them, and re-layouts  12.6 us
    psum x1, blocking collectives, on_device(): lax.psum((jnp.sum(weighted, axis=(0, 2, 3)), jnp.sum(own_flags, axis=0)),...  10.4 us
    psum x1, blocking collectives, on_device(): dweight, dembed = lax.psum((dweight, dembed), 'dp')  7.59 us
    psum x1, blocking collectives, on_device(): lax.psum(jnp.sum(own_flags[:, :, None, None] * centered * centered, axis=...  6.61 us
  transfers between devices with their start and end apart: 3, of which 2 were waited for; matrix products, arithmetic and copies ran while one was open for 4% of the time, Pallas kernels for 0%

commit v1 on v0

v1 whole, which is shorter than its diff:
```python
import math

import jax
import jax.numpy as jnp
from jax import lax
from jax.experimental import pallas as pl
from jax.experimental.pallas import tpu as pltpu
from jax.sharding import PartitionSpec as P

HEADS = 16
LANES = 128
SPAN = 256

field_eps = 1e-05
key_eps = 1e-06
masked_low = -1e30

f32 = jnp.float32
bf16 = jnp.bfloat16


def params(mib):
    return pltpu.CompilerParams(vmem_limit_bytes=mib * 2**20)


def stats_kernel(presence_ref, slot_ref, fields_ref, out_ref):
    own = lax.axis_index("var")
    flag = presence_ref[0, slot_ref[own]].astype(f32)
    values = fields_ref[...].astype(f32)
    cells = values.shape[0] * values.shape[1]
    total = jnp.sum(jnp.sum(values, axis=0, keepdims=True), axis=1, keepdims=True)
    centered = values - total / cells
    squares = jnp.sum(jnp.sum(centered * centered, axis=0, keepdims=True), axis=1, keepdims=True)
    row = lax.broadcasted_iota(jnp.int32, out_ref.shape, 0)
    out_ref[...] = jnp.where(row == 0, total, jnp.where(row == 1, squares, 1.0)) * flag


def token_kernel(stats_ref, fields_ref, weight_ref, embed_ref, tokens_ref, normed_ref, rows, parts):
    patches, pixels = fields_ref.shape
    cells = float(patches * pixels)
    groups = weight_ref.shape[1] // LANES
    samples = stats_ref.shape[0]
    sums = [stats_ref[b, 0:1, :] for b in range(samples)]
    flags = [stats_ref[b, 2:3, :] for b in range(samples)]
    cell_total = jnp.maximum(sum(flags[1:], flags[0]), 1.0) * cells
    mean = sum(sums[1:], sums[0]) / cell_total
    second = jnp.zeros_like(mean)
    for b in range(samples):
        shift = sums[b] / cells - mean
        second = second + stats_ref[b, 1:2, :] + flags[b] * cells * shift * shift
    scale = lax.rsqrt(second / cell_total + field_eps)
    normed = ((fields_ref[...].astype(f32) - mean[:, :pixels]) * scale[:, :pixels]).astype(bf16)
    tokens = jnp.dot(normed, weight_ref[...], preferred_element_type=f32)
    tokens = tokens + embed_ref[...].astype(f32)
    for j in range(groups):
        rows[pl.ds(j, patches, stride=groups), :] = tokens[:, j * LANES : (j + 1) * LANES]
    tokens_ref[...] = rows[...].reshape(tokens_ref.shape).astype(bf16)
    lane = lax.broadcasted_iota(jnp.int32, parts.shape, 1)
    parts[...] = jnp.where(lane == pixels, 1.0, 0.0)
    parts[:, :pixels] = normed.astype(f32)
    half = patches // 2
    for p in range(2):
        normed_ref[p * half : (p + 1) * half, :] = parts[pl.ds(p, half, stride=2), :].astype(bf16)


def head_rows(width):
    row = lax.broadcasted_iota(jnp.int32, (width, LANES), 0)
    lane = lax.broadcasted_iota(jnp.int32, (width, LANES), 1)
    head = row // (width // HEADS)
    return jnp.where((lane % HEADS == head) & (lane < 3 * HEADS), 1.0, 0.0).astype(bf16)


def head_lanes(width):
    row = lax.broadcasted_iota(jnp.int32, (LANES, width), 0)
    lane = lax.broadcasted_iota(jnp.int32, (LANES, width), 1)
    head = lane // (width // HEADS)
    return jnp.where((row % HEADS == head) & (row < 3 * HEADS), 1.0, 0.0).astype(bf16)


def head_sums(values, selector):
    high = values.astype(bf16)
    low = (values - high.astype(f32)).astype(bf16)
    return jnp.dot(high, selector, preferred_element_type=f32) + jnp.dot(
        low, selector, preferred_element_type=f32
    )


def three_parts(values):
    lane = lax.broadcasted_iota(jnp.int32, values.shape, 1)
    high = values.astype(bf16).astype(f32)
    rest = values - high
    middle = rest.astype(bf16).astype(f32)
    low = rest - middle
    parts = jnp.where(lane < HEADS, high, jnp.where(lane < 2 * HEADS, middle, low))
    return parts.astype(bf16)


def mix_kernel(
    presence_ref,
    slot_ref,
    recv_ref,
    key_ref,
    value_ref,
    query_ref,
    grad_ref,
    mixed_ref,
    send_ref,
    arrived,
    tokens,
    keys,
    values,
    key_grad,
    value_grad,
    leaving,
):
    slots, recv_rows, _ = recv_ref.shape
    width = key_ref.shape[0]
    groups = width // LANES
    send_rows = send_ref.shape[1]
    head_dim = width // HEADS
    score_scale = 1.0 / math.sqrt(head_dim)
    pairs = recv_rows // groups
    spans = [slice(c, c + SPAN) for c in range(0, width, SPAN)]
    halves = [slice(p * slots, (p + 1) * slots) for p in range(pairs)]

    arrived[...] = recv_ref[...].astype(f32).reshape(arrived.shape)
    for p in range(pairs):
        for j in range(groups):
            block = arrived[pl.ds(p * groups + j, slots, stride=recv_rows), :]
            tokens[halves[p], j * LANES : (j + 1) * LANES] = block.astype(bf16)

    row = lax.broadcasted_iota(jnp.int32, (LANES, slots), 0)
    lookup = jnp.where(row == slot_ref[...], 1.0, 0.0).astype(bf16)
    present = jnp.broadcast_to(presence_ref[...].astype(f32), (slots, LANES)).astype(bf16)
    present = jnp.dot(present, lookup, preferred_element_type=f32)
    valid = jnp.transpose(present) > 0.5

    query = query_ref[...]
    grad = grad_ref[...].astype(f32)
    selector = head_rows(width)
    spread = head_lanes(width)

    squares = jnp.zeros((pairs * slots, LANES), f32)
    raw = jnp.zeros((pairs * slots, LANES), f32)
    attn_grad = jnp.zeros((pairs * slots, LANES), f32)
    for span in spans:
        block = jnp.dot(tokens[...], key_ref[:, span], preferred_element_type=f32)
        keys[:, span] = block
        squares = squares + head_sums(block * block, selector[span])
        raw = raw + head_sums(block * query[:, span], selector[span])
    for span in spans:
        block = jnp.dot(tokens[...], value_ref[:, span], preferred_element_type=f32)
        values[:, span] = block
        product = jnp.concatenate([block[halves[p]] * grad[p : p + 1, span] for p in range(pairs)], axis=0)
        attn_grad = attn_grad + head_sums(product, selector[span])

    ratio = lax.rsqrt(squares * (1.0 / head_dim) + key_eps)
    scores = raw * ratio * score_scale
    attention, dscore = [], []
    for p in range(pairs):
        part = scores[halves[p]]
        top = jnp.max(jnp.where(valid, part, masked_low), axis=0, keepdims=True)
        weights = jnp.where(valid, jnp.exp(part - top), 0.0)
        weights = weights / jnp.sum(weights, axis=0, keepdims=True)
        change = attn_grad[halves[p]]
        inner = jnp.sum(weights * change, axis=0, keepdims=True)
        attention.append(weights)
        dscore.append(weights * (change - inner))
    attention = jnp.concatenate(attention, axis=0)
    dscore = jnp.concatenate(dscore, axis=0)
    along = dscore * ratio * score_scale
    across = dscore * scores * ratio * ratio * (1.0 / head_dim)
    attention_parts = three_parts(attention)
    along_parts = three_parts(along)
    across_parts = three_parts(across)

    for span in spans:
        weights = jnp.dot(attention_parts, spread[:, span], preferred_element_type=f32)
        first = jnp.dot(along_parts, spread[:, span], preferred_element_type=f32)
        second = jnp.dot(across_parts, spread[:, span], preferred_element_type=f32)
        key_block = keys[:, span]
        key_grad[:, span] = (first * query[:, span] - second * key_block).astype(bf16)
        dquery = jnp.sum(first * key_block, axis=0, keepdims=True)
        for p in range(pairs):
            part = weights[halves[p]]
            value_grad[halves[p], span] = (part * grad[p : p + 1, span]).astype(bf16)
            mixed_ref[p : p + 1, span] = jnp.sum(
                part * values[halves[p], span], axis=0, keepdims=True
            ).astype(bf16)
        for i in range(SPAN // LANES):
            j = span.start // LANES + i
            line = dquery[:, i * LANES : (i + 1) * LANES]
            leaving[pl.ds(pairs * groups + j, slots, stride=send_rows), :] = jnp.broadcast_to(
                line, (slots, LANES)
            )

    contract = (((1,), (1,)), ((), ()))
    for span in spans:
        block = lax.dot_general(key_grad[...], key_ref[span, :], contract, preferred_element_type=f32)
        block = block + lax.dot_general(
            value_grad[...], value_ref[span, :], contract, preferred_element_type=f32
        )
        for p in range(pairs):
            for i in range(SPAN // LANES):
                j = span.start // LANES + i
                leaving[pl.ds(p * groups + j, slots, stride=send_rows), :] = block[
                    halves[p], i * LANES : (i + 1) * LANES
                ]
    send_ref[...] = leaving[...].reshape(send_ref.shape).astype(bf16)


def grad_kernel(recv_ref, normed_ref, out_ref, arrived, grads):
    owners, recv_rows, _ = recv_ref.shape
    width = grads.shape[1]
    groups = width // LANES
    pairs = recv_rows // groups - 1
    pixels = out_ref.shape[0] // groups - 2
    blocks = recv_ref[...].astype(f32)
    arrived[...] = blocks.reshape(arrived.shape)
    dquery = jnp.sum(blocks[:, pairs * groups :, :], axis=0)
    for p in range(pairs):
        for j in range(groups):
            block = arrived[pl.ds(p * groups + j, owners, stride=recv_rows), :]
            grads[p * owners : (p + 1) * owners, j * LANES : (j + 1) * LANES] = block.astype(bf16)
    sums = lax.dot_general(
        normed_ref[...], grads[...], (((0,), (0,)), ((), ())), preferred_element_type=f32
    )
    for j in range(groups):
        lanes = slice(j * LANES, (j + 1) * LANES)
        out_ref[j * pixels : (j + 1) * pixels, :] = sums[:pixels, lanes]
        out_ref[groups * pixels + j : groups * pixels + j + 1, :] = sums[pixels : pixels + 1, lanes]
    out_ref[groups * (pixels + 1) :, :] = dquery


def total_kernel(parts_ref, weight_ref, embed_ref, query_ref):
    pixels, width = weight_ref.shape
    groups = width // LANES
    total = (parts_ref[0] + parts_ref[1]) + (parts_ref[2] + parts_ref[3])
    for j in range(groups):
        lanes = slice(j * LANES, (j + 1) * LANES)
        weight_ref[:, lanes] = total[j * pixels : (j + 1) * pixels]
        embed_ref[:, lanes] = total[groups * pixels + j : groups * pixels + j + 1]
        query_ref[:, lanes] = total[groups * (pixels + 1) + j : groups * (pixels + 1) + j + 1]


smem = pl.BlockSpec(memory_space=pltpu.SMEM)
vmem = pl.BlockSpec(memory_space=pltpu.VMEM)


def on_device(
    fields, presence, slot_var, patch_weight, var_embed, query, key_weight, value_weight, out_grad
):
    var_count = lax.axis_size("var")
    _, _, patches, pixels = fields.shape
    width = key_weight.shape[0]
    groups = width // LANES
    slots = slot_var.shape[0]
    pairs = patches // var_count
    rows = pairs * groups
    fields = fields.reshape(patches, pixels)

    stats = pl.pallas_call(
        stats_kernel,
        out_shape=jax.ShapeDtypeStruct((8, LANES), f32),
        in_specs=[smem, smem, vmem],
        out_specs=vmem,
        name="stats",
    )(presence, slot_var, fields)
    stats = lax.all_gather(stats, "dp")

    tokens, normed = pl.pallas_call(
        token_kernel,
        out_shape=(
            jax.ShapeDtypeStruct((var_count, rows, LANES), bf16),
            jax.ShapeDtypeStruct((patches, LANES), bf16),
        ),
        in_specs=[vmem] * 4,
        out_specs=(vmem, vmem),
        scratch_shapes=[pltpu.VMEM((patches * groups, LANES), f32), pltpu.VMEM((patches, LANES), f32)],
        compiler_params=params(16),
        name="tokens",
    )(stats, fields, patch_weight.reshape(pixels, width), var_embed)
    gathered = lax.all_to_all(tokens, "var", split_axis=0, concat_axis=0, tiled=True)

    mixed, outgoing = pl.pallas_call(
        mix_kernel,
        out_shape=(
            jax.ShapeDtypeStruct((pairs, width), bf16),
            jax.ShapeDtypeStruct((slots, rows + groups, LANES), bf16),
        ),
        in_specs=[vmem] * 7,
        out_specs=(vmem, vmem),
        scratch_shapes=[
            pltpu.VMEM((slots * rows, LANES), f32),
            pltpu.VMEM((pairs * slots, width), bf16),
            pltpu.VMEM((pairs * slots, width), f32),
            pltpu.VMEM((pairs * slots, width), f32),
            pltpu.VMEM((pairs * slots, width), bf16),
            pltpu.VMEM((pairs * slots, width), bf16),
            pltpu.VMEM((slots * (rows + groups), LANES), f32),
        ],
        compiler_params=params(32),
        name="mix",
    )(
        presence,
        slot_var.reshape(1, slots),
        gathered,
        key_weight,
        value_weight,
        query.reshape(1, width),
        out_grad.reshape(pairs, width),
    )
    returned = lax.all_to_all(outgoing, "var", split_axis=0, concat_axis=0, tiled=True)

    parts = pl.pallas_call(
        grad_kernel,
        out_shape=jax.ShapeDtypeStruct((groups * (pixels + 2), LANES), f32),
        in_specs=[vmem, vmem],
        out_specs=vmem,
        scratch_shapes=[
            pltpu.VMEM((var_count * (rows + groups), LANES), f32),
            pltpu.VMEM((patches, width), bf16),
        ],
        compiler_params=params(16),
        name="grads",
    )(returned, normed)
    parts = lax.all_gather(parts, "dp")

    dweight, dembed, dquery = pl.pallas_call(
        total_kernel,
        out_shape=(
            jax.ShapeDtypeStruct((pixels, width), f32),
            jax.ShapeDtypeStruct((1, width), f32),
            jax.ShapeDtypeStruct((1, width), f32),
        ),
        in_specs=[vmem],
        out_specs=(vmem, vmem, vmem),
        name="totals",
    )(parts)
    return (
        mixed.reshape(1, pairs, width),
        dweight.reshape(1, pixels, width),
        dembed,
        dquery.reshape(width),
    )


def solution(mesh):
    return jax.shard_map(
        on_device,
        mesh=mesh,
        in_specs=(
            P("dp", "var", None, None),
            P("dp", None),
            P(),
            P("var", None, None),
            P("var", None),
            P(),
            P(),
            P(),
            P("dp", "var", None),
        ),
        out_specs=(P("dp", "var", None), P("var", None, None), P("var", None), P()),
        check_vma=False,
    )
```

time: 309 us -> 115 us (0.37)
  waiting for transfers between devices: 52 us -> 0 us
  local copies, waits for them, and re-layouts: 45.8 us -> 9.58 us
  blocking collectives: 123 us -> 92.9 us
  starting transfers between devices: 28.3 us -> 0 us
  other arithmetic: 28 us -> 0 us
  between operations: 17 us -> 0.66 us
  matrix products: 13.1 us -> 0 us
  Pallas kernels: 0 us -> 10.1 us
    psum x4 -> x0, blocking collectives: 123 us -> none  [the longest x1 98.2 us: on_device(): dquery = lax.psum(dquery.reshape(model_width), ('var', 'dp'))]
    all_to_all x0 -> x2, blocking collectives: none -> 72 us  [the longest x1 40.9 us: on_device(): lax.all_to_all(tokens, 'var', split_axis=0, concat_axis=0, tiled=True)]
    psum x1 -> x0, waiting for transfers between devices: 36.6 us -> none  [on_device(): dweight, dembed = lax.psum((dweight, dembed), 'dp')]
    all_to_all x2 -> x0, starting transfers between devices: 28.2 us -> none  [the longest x1 21.8 us: on_device(): lax.all_to_all(tokens, 'var', split_axis=2, concat_axis=1, tiled=True)]
    all_gather x0 -> x2, blocking collectives: none -> 20.9 us  [the longest x1 10.6 us: on_device(): parts = lax.all_gather(parts, 'dp')]
    all_to_all x2 -> x0, waiting for transfers between devices: 15.4 us -> none  [the longest x1 15.4 us: on_device(): lax.all_to_all(tokens, 'var', split_axis=2, concat_axis=1, tiled=True)]
    mul x6 -> x0, local copies, waits for them, and re-layouts: 14.1 us -> none  [the longest x2 4.73 us: token_grads(): norm_grad = dscore[..., None] * query_heads * score_scale]
    reduce_sum x8 -> x0, other arithmetic: 13.8 us -> none  [the longest x1 5.96 us: token_grads(): jnp.mean(norm_grad * normed_keys, axis=-1, keepdims=True)]
  transfers between devices with their start and end apart: 3 -> 0, of which waited for: 2 -> 0; matrix products, arithmetic and copies ran while one was open for 4% -> 0% of each run, Pallas kernels for 0% -> 0%
where the time goes in v1:
time: 115 us; the launch traced here: 113 us
  blocking collectives  92.9 us (81%)
  Pallas kernels  10.1 us (9%)
  local copies, waits for them, and re-layouts  9.58 us (8%)
    all_to_all x1, blocking collectives, on_device(): lax.all_to_all(tokens, 'var', split_axis=0, concat_axis=0, tiled=True)  40.9 us
    all_to_all x1, blocking collectives, on_device(): lax.all_to_all(outgoing, 'var', split_axis=0, concat_axis=0, tiled=True)  31.1 us
    all_gather x1, blocking collectives, on_device(): parts = lax.all_gather(parts, 'dp')  10.6 us
    all_gather x1, blocking collectives, on_device(): stats = lax.all_gather(stats, 'dp')  10.3 us
    unnamed x19, local copies, waits for them, and re-layouts  9.58 us
    pallas_call x1, Pallas kernels, on_device(): pl.pallas_call(mix_kernel, out_shape=(jax.ShapeDtypeStruct((pairs, width)...  5.9 us

profile of v1, /device:TPU:1, one launch (start us, length us, event | category | flops | bytes accessed | tf_op | source)
XLA Modules:
  0.0 113.2 jit_solution(8444178541020425583)
XLA Ops:
  0.6 1.4 %copy.13 = bf16[1,1,256,16]{3,2,1,0:T(8,128)(2,1)} copy(bf16[1,1,256,16]{2,3,1,0:T(8,128)(2,1)} %param.9) | data formatting | bytes 16384 | tf_op args[0]
  2.1 1.7 %stats.1 = f32[8,128]{1,0:T(8,128)} custom-call(s32[1,128]{1,0:T(1,128)} %presence_ref.3, s32[128]{0:T(128)} %slot_ref.1, bf16[256,16]{1,0:T(8,128)(2,1)} %bitcast.10), custom_call_target="tpu_custom_call" | custom-call | tf_op jit(solution)/shard_map/stats/pallas_call | solution.py:262
  3.7 10.3 %all-gather = f32[32,128]{1,0:T(8,128)S(1)} all-gather(f32[8,128]{1,0:T(8,128)} %stats.1), channel_id=2, replica_groups=mesh['var'=128,'dp'=4] {'dp'}, dimensions={0}, use_global_device_ids=true | all-gather | bytes 20480 | tf_op jit(solution)/shard_map/all_gather | solution.py:269
  14.1 0.0 copy-start.2
  14.1 0.8 copy-done.2
  14.9 0.0 copy-start.3
  14.9 0.8 copy-done.3
  15.7 0.0 copy-start.4
  15.7 0.7 copy-done.4
  16.4 0.4 tokens.1
  16.8 40.9 %all_to_all.10.recv_ref = bf16[128,16,128]{2,1,0:T(8,128)(2,1)S(1)} all-to-all(bf16[128,16,128]{2,1,0:T(8,128)(2,1)S(1)} %get-tuple-element.11), channel_id=1, replica_groups=mesh['var'=128,'dp'=4] {'var'}, dimensions={0} | all-to-all | bytes 1048576 | tf_op jit(solution)/shard_map/all_to_all | solution.py:283
  57.6 0.0 copy-start
  57.6 1.6 %copy-done = bf16[1024,1024]{1,0:T(8,128)(2,1)S(1)} copy-done((bf16[1024,1024]{1,0:T(8,128)(2,1)S(1)}, bf16[1024,1024]{1,0:T(8,128)(2,1)}, u32[]{:S(2)}) %copy-start) | copy-done | bytes 2097176
  59.2 0.0 copy-start.1
  59.2 1.6 %copy-done.1 = bf16[1024,1024]{1,0:T(8,128)(2,1)S(1)} copy-done((bf16[1024,1024]{1,0:T(8,128)(2,1)S(1)}, bf16[1024,1024]{1,0:T(8,128)(2,1)}, u32[]{:S(2)}) %copy-start.1) | copy-done | bytes 2097176
  60.8 0.0 copy-start.5
  60.8 0.7 copy-done.5
  61.5 0.0 copy-start.6
  61.5 0.7 copy-done.6
  62.2 0.0 copy-start.7
  62.2 0.7 copy-done.7
  62.8 0.0 copy-start.8
  62.8 0.7 copy-done.8
  63.5 5.9 %mix.1 = (bf16[2,1024]{1,0:T(2,128)(2,1)}, bf16[128,24,128]{2,1,0:T(8,128)(2,1)S(1)}) custom-call(s32[1,128]{1,0:T(1,128)S(1)} %copy-done.7, s32[1,128]{1,0:T(1,128)S(1)} %bitcast.16, bf16[128,16,128]{2,1,0:T(8,128)(2,1)S(1)} %all_to_all.10.recv_ref, bf16[1024,1024]{1,0:T(8,128)(2,1)S(1)} %copy-done, bf16[1024,1024]{1,0:T(8,128)(2,1)S(1)} %copy-done.1, ...), custom_call_target="tpu_custom_call" | custom-call | tf_op jit(solution)/shard_map/mix/pallas_call | solution.py:285
  69.4 31.1 %all_to_all.11.recv_ref = bf16[128,24,128]{2,1,0:T(8,128)(2,1)S(1)} all-to-all(bf16[128,24,128]{2,1,0:T(8,128)(2,1)S(1)} %get-tuple-element.13), channel_id=1, replica_groups=mesh['var'=128,'dp'=4] {'var'}, dimensions={0} | all-to-all | bytes 1572864 | tf_op jit(solution)/shard_map/all_to_all | solution.py:313
  100.5 0.5 grads.1
  101.0 10.6 %all-gather.1 = f32[576,128]{1,0:T(8,128)} all-gather(f32[144,128]{1,0:T(8,128)S(1)} %grads.1), channel_id=3, replica_groups=mesh['var'=128,'dp'=4] {'dp'}, dimensions={0}, use_global_device_ids=true | all-gather | bytes 368640 | tf_op jit(solution)/shard_map/all_gather | solution.py:327
  111.6 1.6 %totals.1 = (f32[16,1024]{1,0:T(8,128)}, f32[1,1024]{1,0:T(1,128)}, f32[1,1024]{1,0:T(1,128)}) custom-call(f32[4,144,128]{2,1,0:T(8,128)} %bitcast.17), custom_call_target="tpu_custom_call" | custom-call | tf_op jit(solution)/shard_map/totals/pallas_call | solution.py:329
Async XLA Ops:
  14.1 0.8 copy-start.2
  14.9 0.8 copy-start.3
  15.7 0.7 copy-start.4
  57.6 1.6 %copy-start = (bf16[1024,1024]{1,0:T(8,128)(2,1)S(1)}, bf16[1024,1024]{1,0:T(8,128)(2,1)}, u32[]{:S(2)}) copy-start(bf16[1024,1024]{1,0:T(8,128)(2,1)} %key_ref.1) | copy-start | bytes 6291460
  59.2 1.6 %copy-start.1 = (bf16[1024,1024]{1,0:T(8,128)(2,1)S(1)}, bf16[1024,1024]{1,0:T(8,128)(2,1)}, u32[]{:S(2)}) copy-start(bf16[1024,1024]{1,0:T(8,128)(2,1)} %value_ref.1) | copy-start | bytes 6291460
  60.8 0.7 copy-start.5
  61.5 0.7 copy-start.6
  62.2 0.7 copy-start.7
  62.8 0.7 copy-start.8

commit v2 on v1

--- a/solution.py
+++ b/solution.py
@@ -10,6 +10,7 @@
 HEADS = 16
 LANES = 128
 SPAN = 256
+FLOPS, BYTES = 6_000_000_000, 2_000_000
 
 field_eps = 1e-05
 key_eps = 1e-06
@@ -23,41 +24,81 @@
     return pltpu.CompilerParams(vmem_limit_bytes=mib * 2**20)
 
 
-def stats_kernel(presence_ref, slot_ref, fields_ref, out_ref):
+def stats_kernel(
+    presence_ref,
+    slot_ref,
+    fields_ref,
+    weight_ref,
+    embed_ref,
+    presence_row,
+    slot_row,
+    query_ref,
+    grad_ref,
+    stats_ref,
+    fields_out,
+    weight_out,
+    embed_out,
+    presence_out,
+    slot_out,
+    query_out,
+    grad_out,
+    arrivals,
+):
+    moves = [
+        pltpu.make_async_copy(source, target, arrivals.at[i])
+        for i, (source, target) in enumerate(
+            (
+                (fields_ref, fields_out),
+                (weight_ref, weight_out),
+                (embed_ref, embed_out),
+                (presence_row, presence_out),
+                (slot_row, slot_out),
+                (query_ref, query_out),
+                (grad_ref, grad_out),
+            )
+        )
+    ]
+    for move in moves:
+        move.start()
     own = lax.axis_index("var")
     flag = presence_ref[0, slot_ref[own]].astype(f32)
-    values = fields_ref[...].astype(f32)
+    moves[0].wait()
+    values = fields_out[...].astype(f32)
     cells = values.shape[0] * values.shape[1]
     total = jnp.sum(jnp.sum(values, axis=0, keepdims=True), axis=1, keepdims=True)
     centered = values - total / cells
     squares = jnp.sum(jnp.sum(centered * centered, axis=0, keepdims=True), axis=1, keepdims=True)
-    row = lax.broadcasted_iota(jnp.int32, out_ref.shape, 0)
-    out_ref[...] = jnp.where(row == 0, total, jnp.where(row == 1, squares, 1.0)) * flag
+    lane = lax.broadcasted_iota(jnp.int32, stats_ref.shape, 1)
+    stats_ref[...] = jnp.where(lane == 0, total, jnp.where(lane == 1, squares, 1.0)) * flag
+    for move in moves[1:]:
+        move.wait()
 
 
 def token_kernel(stats_ref, fields_ref, weight_ref, embed_ref, tokens_ref, normed_ref, rows, parts):
-    patches, pixels = fields_ref.shape
+    pixels, patches = fields_ref.shape
     cells = float(patches * pixels)
     groups = weight_ref.shape[1] // LANES
     samples = stats_ref.shape[0]
-    sums = [stats_ref[b, 0:1, :] for b in range(samples)]
-    flags = [stats_ref[b, 2:3, :] for b in range(samples)]
+    sums = [stats_ref[b, :, 0:1] for b in range(samples)]
+    flags = [stats_ref[b, :, 2:3] for b in range(samples)]
     cell_total = jnp.maximum(sum(flags[1:], flags[0]), 1.0) * cells
     mean = sum(sums[1:], sums[0]) / cell_total
     second = jnp.zeros_like(mean)
     for b in range(samples):
         shift = sums[b] / cells - mean
-        second = second + stats_ref[b, 1:2, :] + flags[b] * cells * shift * shift
+        second = second + stats_ref[b, :, 1:2] + flags[b] * cells * shift * shift
     scale = lax.rsqrt(second / cell_total + field_eps)
-    normed = ((fields_ref[...].astype(f32) - mean[:, :pixels]) * scale[:, :pixels]).astype(bf16)
-    tokens = jnp.dot(normed, weight_ref[...], preferred_element_type=f32)
+    row = lax.broadcasted_iota(jnp.int32, (LANES, patches), 0)
+    upright = jnp.concatenate(
+        [(fields_ref[...].astype(f32) - mean) * scale, jnp.zeros((LANES - pixels, patches), f32)], axis=0
+    )
+    normed = jnp.transpose(jnp.where(row == pixels, 1.0, upright))
+    parts[...] = normed.astype(bf16).astype(f32)
+    tokens = jnp.dot(normed[:, :pixels].astype(bf16), weight_ref[...], preferred_element_type=f32)
     tokens = tokens + embed_ref[...].astype(f32)
     for j in range(groups):
         rows[pl.ds(j, patches, stride=groups), :] = tokens[:, j * LANES : (j + 1) * LANES]
     tokens_ref[...] = rows[...].reshape(tokens_ref.shape).astype(bf16)
-    lane = lax.broadcasted_iota(jnp.int32, parts.shape, 1)
-    parts[...] = jnp.where(lane == pixels, 1.0, 0.0)
-    parts[:, :pixels] = normed.astype(f32)
     half = patches // 2
     for p in range(2):
         normed_ref[p * half : (p + 1) * half, :] = parts[pl.ds(p, half, stride=2), :].astype(bf16)
@@ -214,7 +255,8 @@
     width = grads.shape[1]
     groups = width // LANES
     pairs = recv_rows // groups - 1
-    pixels = out_ref.shape[0] // groups - 2
+    copies, out_rows, _ = out_ref.shape
+    pixels = out_rows // groups - 2
     blocks = recv_ref[...].astype(f32)
     arrived[...] = blocks.reshape(arrived.shape)
     dquery = jnp.sum(blocks[:, pairs * groups :, :], axis=0)
@@ -227,9 +269,13 @@
     )
     for j in range(groups):
         lanes = slice(j * LANES, (j + 1) * LANES)
-        out_ref[j * pixels : (j + 1) * pixels, :] = sums[:pixels, lanes]
-        out_ref[groups * pixels + j : groups * pixels + j + 1, :] = sums[pixels : pixels + 1, lanes]
-    out_ref[groups * (pixels + 1) :, :] = dquery
+        for c in range(copies):
+            out_ref[c, j * pixels : (j + 1) * pixels, :] = sums[:pixels, lanes]
+            out_ref[c, groups * pixels + j : groups * pixels + j + 1, :] = sums[
+                pixels : pixels + 1, lanes
+            ]
+    for c in range(copies):
+        out_ref[c, groups * (pixels + 1) :, :] = dquery
 
 
 def total_kernel(parts_ref, weight_ref, embed_ref, query_ref):
@@ -245,6 +291,7 @@
 
 smem = pl.BlockSpec(memory_space=pltpu.SMEM)
 vmem = pl.BlockSpec(memory_space=pltpu.VMEM)
+hbm = pl.BlockSpec(memory_space=pltpu.HBM)
 
 
 def on_device(
@@ -257,15 +304,29 @@
     slots = slot_var.shape[0]
     pairs = patches // var_count
     rows = pairs * groups
-    fields = fields.reshape(patches, pixels)
-
-    stats = pl.pallas_call(
+    samples = lax.axis_size("dp")
+    fixed = tuple(
+        pltpu.with_memory_space_constraint(a, pltpu.HBM)
+        for a in (
+            jnp.transpose(fields.reshape(patches, pixels)),
+        patch_weight.reshape(pixels, width),
+        var_embed,
+        presence,
+        slot_var.reshape(1, slots),
+        query.reshape(1, width),
+        out_grad.reshape(pairs, width),
+        )
+    )
+
+    stats, fields, patch_weight, var_embed, present, slot_row, query_row, grad_rows = pl.pallas_call(
         stats_kernel,
-        out_shape=jax.ShapeDtypeStruct((8, LANES), f32),
-        in_specs=[smem, smem, vmem],
-        out_specs=vmem,
+        out_shape=(jax.ShapeDtypeStruct((1, LANES), f32),)
+        + tuple(pltpu.VMEM(a.shape, a.dtype) for a in fixed),
+        in_specs=[smem, smem] + [hbm] * len(fixed),
+        out_specs=[vmem] * (1 + len(fixed)),
+        scratch_shapes=[pltpu.SemaphoreType.DMA((len(fixed),))],
         name="stats",
-    )(presence, slot_var, fields)
+    )(presence, slot_var, *fixed)
     stats = lax.all_gather(stats, "dp")
 
     tokens, normed = pl.pallas_call(
@@ -278,8 +339,9 @@
         out_specs=(vmem, vmem),
         scratch_shapes=[pltpu.VMEM((patches * groups, LANES), f32), pltpu.VMEM((patches, LANES), f32)],
         compiler_params=params(16),
+        cost_estimate=pl.CostEstimate(flops=FLOPS, bytes_accessed=BYTES, transcendentals=0),
         name="tokens",
-    )(stats, fields, patch_weight.reshape(pixels, width), var_embed)
+    )(stats, fields, patch_weight, var_embed)
     gathered = lax.all_to_all(tokens, "var", split_axis=0, concat_axis=0, tiled=True)
 
     mixed, outgoing = pl.pallas_call(
@@ -301,20 +363,12 @@
         ],
         compiler_params=params(32),
         name="mix",
-    )(
-        presence,
-        slot_var.reshape(1, slots),
-        gathered,
-        key_weight,
-        value_weight,
-        query.reshape(1, width),
-        out_grad.reshape(pairs, width),
-    )
+    )(present, slot_row, gathered, key_weight, value_weight, query_row, grad_rows)
     returned = lax.all_to_all(outgoing, "var", split_axis=0, concat_axis=0, tiled=True)
 
     parts = pl.pallas_call(
         grad_kernel,
-        out_shape=jax.ShapeDtypeStruct((groups * (pixels + 2), LANES), f32),
+        out_shape=jax.ShapeDtypeStruct((samples, groups * (pixels + 2), LANES), f32),
         in_specs=[vmem, vmem],
         out_specs=vmem,
         scratch_shapes=[
@@ -324,7 +378,7 @@
         compiler_params=params(16),
         name="grads",
     )(returned, normed)
-    parts = lax.all_gather(parts, "dp")
+    parts = lax.all_to_all(parts, "dp", split_axis=0, concat_axis=0, tiled=True)
 
     dweight, dembed, dquery = pl.pallas_call(
         total_kernel,

time: 115 us -> 102 us (0.89); the launches traced: 113 us -> 102 us
  local copies, waits for them, and re-layouts: 9.58 us -> 0.01 us
  blocking collectives: 92.9 us -> 90.2 us
    all_gather x1 -> x0, blocking collectives: 10.6 us -> none  [on_device(): parts = lax.all_gather(parts, 'dp')]
    all_to_all x0 -> x1, blocking collectives: none -> 10.3 us  [on_device(): parts = lax.all_to_all(parts, 'dp', split_axis=0, concat_axis=0, tiled=True)]
    unnamed x19 -> x4, local copies, waits for them, and re-layouts: 9.58 us -> 0.01 us
    all_gather x1, blocking collectives: 10.3 us -> 8.65 us  [on_device(): stats = lax.all_gather(stats, 'dp')]
where the time goes in v2:
time: 102 us
  blocking collectives  90.2 us (88%)
  Pallas kernels  10.9 us (11%)
    all_to_all x1, blocking collectives, on_device(): lax.all_to_all(tokens, 'var', split_axis=0, concat_axis=0, tiled=True)  40.1 us
    all_to_all x1, blocking collectives, on_device(): lax.all_to_all(outgoing, 'var', split_axis=0, concat_axis=0, tiled=True)  31.1 us
    all_to_all x1, blocking collectives, on_device(): parts = lax.all_to_all(parts, 'dp', split_axis=0, concat_axis=0, tiled=True)  10.3 us
    all_gather x1, blocking collectives, on_device(): stats = lax.all_gather(stats, 'dp')  8.65 us
    pallas_call x1, Pallas kernels, on_device(): pl.pallas_call(mix_kernel, out_shape=(jax.ShapeDtypeStruct((pairs, width)...  5.9 us
    pallas_call x1, Pallas kernels, on_device(): pl.pallas_call(stats_kernel, out_shape=(jax.ShapeDtypeStruct((1, LANES),...  2.13 us

profile of v2, /device:TPU:1, one launch (start us, length us, event | category | flops | bytes accessed | tf_op | source)
XLA Modules:
  0.0 101.8 jit_solution(17736990453405468089)
XLA Ops:
  0.6 2.1 %stats.1 = (f32[1,128]{1,0:T(1,128)}, bf16[16,256]{1,0:T(8,128)(2,1)S(1)}, bf16[16,1024]{1,0:T(8,128)(2,1)S(1)}, bf16[1,1024]{1,0:T(2,128)(2,1)S(1)}, s32[1,128]...) custom-call(s32[1,128]{1,0:T(1,128)} %presence_row.1, s32[128]{0:T(128)} %slot_ref.1, ...), custom_call_target="tpu_custom_call" | custom-call | tf_op jit(solution)/shard_map/stats/pallas_call | solution.py:321
  2.8 8.6 %all-gather.1.stats_ref = f32[4,1,128]{2,1,0:T(1,128)S(1)} all-gather(f32[1,1,128]{2,1,0:T(1,128)} %bitcast.16), channel_id=2, replica_groups=mesh['var'=128,'dp'=4] {'dp'}, dimensions={0}, use_global_device_ids=true | all-gather | bytes 2560 | tf_op jit(solution)/shard_map/all_gather | solution.py:330
  11.4 0.0 copy-start
  11.4 0.0 copy-start.1
  11.4 0.7 tokens.1
  12.2 40.1 %all_to_all.15.recv_ref = bf16[128,16,128]{2,1,0:T(8,128)(2,1)S(1)} all-to-all(bf16[128,16,128]{2,1,0:T(8,128)(2,1)S(1)} %get-tuple-element.25), channel_id=1, replica_groups=mesh['var'=128,'dp'=4] {'var'}, dimensions={0} | all-to-all | bytes 1048576 | tf_op jit(solution)/shard_map/all_to_all | solution.py:345
  52.3 0.0 copy-done
  52.3 0.0 copy-done.1
  52.3 5.9 %mix.1 = (bf16[2,1024]{1,0:T(2,128)(2,1)}, bf16[128,24,128]{2,1,0:T(8,128)(2,1)S(1)}) custom-call(s32[1,128]{1,0:T(1,128)S(1)} %get-tuple-element.19.presence_ref, s32[1,128]{1,0:T(1,128)S(1)} %get-tuple-element.20.slot_ref, bf16[128,16,128]{2,1,0:T(8,128)(2,1)S(1)} %all_to_all.15.recv_ref, bf16[1024,1024]{1,0:T(8,128)(2,1)S(1)} %copy-done, ...), custom_call_target="tpu_custom_call" | custom-call | tf_op jit(solution)/shard_map/mix/pallas_call | solution.py:347
  58.2 31.1 %all_to_all.16.recv_ref = bf16[128,24,128]{2,1,0:T(8,128)(2,1)S(1)} all-to-all(bf16[128,24,128]{2,1,0:T(8,128)(2,1)S(1)} %get-tuple-element.29), channel_id=1, replica_groups=mesh['var'=128,'dp'=4] {'var'}, dimensions={0} | all-to-all | bytes 1572864 | tf_op jit(solution)/shard_map/all_to_all | solution.py:367
  89.3 0.5 grads.1
  89.8 10.3 %all_to_all.17.parts_ref = f32[4,144,128]{2,1,0:T(8,128)} all-to-all(f32[4,144,128]{2,1,0:T(8,128)S(1)} %grads.1), channel_id=1, replica_groups=mesh['var'=128,'dp'=4] {'dp'}, dimensions={0} | all-to-all | bytes 589824 | tf_op jit(solution)/shard_map/all_to_all | solution.py:381
  100.2 1.6 %totals.1 = (f32[16,1024]{1,0:T(8,128)}, f32[1,1024]{1,0:T(1,128)}, f32[1,1024]{1,0:T(1,128)}) custom-call(f32[4,144,128]{2,1,0:T(8,128)} %all_to_all.17.parts_ref), custom_call_target="tpu_custom_call" | custom-call | tf_op jit(solution)/shard_map/totals/pallas_call | solution.py:383
Async XLA Ops:
  11.4 40.9 %copy-start = (bf16[1024,1024]{1,0:T(8,128)(2,1)S(1)}, bf16[1024,1024]{1,0:T(8,128)(2,1)}, u32[]{:S(2)}) copy-start(bf16[1024,1024]{1,0:T(8,128)(2,1)} %key_ref.1) | copy-start | bytes 6291460
  11.4 40.9 %copy-start.1 = (bf16[1024,1024]{1,0:T(8,128)(2,1)S(1)}, bf16[1024,1024]{1,0:T(8,128)(2,1)}, u32[]{:S(2)}) copy-start(bf16[1024,1024]{1,0:T(8,128)(2,1)} %value_ref.1) | copy-start | bytes 6291460

commit v3 on v2

--- a/solution.py
+++ b/solution.py
@@ -10,7 +10,6 @@
 HEADS = 16
 LANES = 128
 SPAN = 256
-FLOPS, BYTES = 6_000_000_000, 2_000_000
 
 field_eps = 1e-05
 key_eps = 1e-06
@@ -25,13 +24,11 @@
 
 
 def stats_kernel(
-    presence_ref,
-    slot_ref,
     fields_ref,
     weight_ref,
     embed_ref,
-    presence_row,
-    slot_row,
+    presence_ref,
+    slot_ref,
     query_ref,
     grad_ref,
     stats_ref,
@@ -48,11 +45,11 @@
         pltpu.make_async_copy(source, target, arrivals.at[i])
         for i, (source, target) in enumerate(
             (
+                (presence_ref, presence_out),
+                (slot_ref, slot_out),
                 (fields_ref, fields_out),
                 (weight_ref, weight_out),
                 (embed_ref, embed_out),
-                (presence_row, presence_out),
-                (slot_row, slot_out),
                 (query_ref, query_out),
                 (grad_ref, grad_out),
             )
@@ -60,21 +57,25 @@
     ]
     for move in moves:
         move.start()
-    own = lax.axis_index("var")
-    flag = presence_ref[0, slot_ref[own]].astype(f32)
+    lane = lax.broadcasted_iota(jnp.int32, stats_ref.shape, 1)
     moves[0].wait()
+    moves[1].wait()
+    slot = jnp.where(lane == lax.axis_index("var"), slot_out[...], 0)
+    slot = jnp.sum(slot.astype(f32), axis=1, keepdims=True).astype(jnp.int32)
+    flag = jnp.where(lane == slot, presence_out[...], 0).astype(f32)
+    flag = jnp.sum(flag, axis=1, keepdims=True)
+    moves[2].wait()
     values = fields_out[...].astype(f32)
     cells = values.shape[0] * values.shape[1]
     total = jnp.sum(jnp.sum(values, axis=0, keepdims=True), axis=1, keepdims=True)
     centered = values - total / cells
     squares = jnp.sum(jnp.sum(centered * centered, axis=0, keepdims=True), axis=1, keepdims=True)
-    lane = lax.broadcasted_iota(jnp.int32, stats_ref.shape, 1)
     stats_ref[...] = jnp.where(lane == 0, total, jnp.where(lane == 1, squares, 1.0)) * flag
-    for move in moves[1:]:
+    for move in moves[3:]:
         move.wait()
 
 
-def token_kernel(stats_ref, fields_ref, weight_ref, embed_ref, tokens_ref, normed_ref, rows, parts):
+def token_kernel(stats_ref, fields_ref, weight_ref, embed_ref, tokens_ref, normed_ref, rows):
     pixels, patches = fields_ref.shape
     cells = float(patches * pixels)
     groups = weight_ref.shape[1] // LANES
@@ -88,27 +89,22 @@
         shift = sums[b] / cells - mean
         second = second + stats_ref[b, :, 1:2] + flags[b] * cells * shift * shift
     scale = lax.rsqrt(second / cell_total + field_eps)
-    row = lax.broadcasted_iota(jnp.int32, (LANES, patches), 0)
-    upright = jnp.concatenate(
-        [(fields_ref[...].astype(f32) - mean) * scale, jnp.zeros((LANES - pixels, patches), f32)], axis=0
+    normed = ((fields_ref[...].astype(f32) - mean) * scale).astype(bf16)
+    tokens = lax.dot_general(
+        normed, weight_ref[...], (((0,), (0,)), ((), ())), preferred_element_type=f32
     )
-    normed = jnp.transpose(jnp.where(row == pixels, 1.0, upright))
-    parts[...] = normed.astype(bf16).astype(f32)
-    tokens = jnp.dot(normed[:, :pixels].astype(bf16), weight_ref[...], preferred_element_type=f32)
     tokens = tokens + embed_ref[...].astype(f32)
     for j in range(groups):
         rows[pl.ds(j, patches, stride=groups), :] = tokens[:, j * LANES : (j + 1) * LANES]
     tokens_ref[...] = rows[...].reshape(tokens_ref.shape).astype(bf16)
+    row = lax.broadcasted_iota(jnp.int32, (normed_ref.shape[0] - pixels, patches), 0)
+    padded = jnp.concatenate([normed.astype(f32), jnp.where(row == 0, 1.0, 0.0)], axis=0)
+    row = lax.broadcasted_iota(jnp.int32, (patches, patches), 0)
+    lane = lax.broadcasted_iota(jnp.int32, (patches, patches), 1)
     half = patches // 2
-    for p in range(2):
-        normed_ref[p * half : (p + 1) * half, :] = parts[pl.ds(p, half, stride=2), :].astype(bf16)
-
-
-def head_rows(width):
-    row = lax.broadcasted_iota(jnp.int32, (width, LANES), 0)
-    lane = lax.broadcasted_iota(jnp.int32, (width, LANES), 1)
-    head = row // (width // HEADS)
-    return jnp.where((lane % HEADS == head) & (lane < 3 * HEADS), 1.0, 0.0).astype(bf16)
+    source = jnp.where(lane < half, 2 * lane, 2 * (lane - half) + 1)
+    order = jnp.where(row == source, 1.0, 0.0).astype(bf16)
+    normed_ref[...] = jnp.dot(padded.astype(bf16), order, preferred_element_type=f32).astype(bf16)
 
 
 def head_lanes(width):
@@ -118,22 +114,24 @@
     return jnp.where((row % HEADS == head) & (row < 3 * HEADS), 1.0, 0.0).astype(bf16)
 
 
-def head_sums(values, selector):
-    high = values.astype(bf16)
-    low = (values - high.astype(f32)).astype(bf16)
-    return jnp.dot(high, selector, preferred_element_type=f32) + jnp.dot(
-        low, selector, preferred_element_type=f32
-    )
+def head_sums(values, sums_ref, first, slots, head_dim):
+    for p in range(sums_ref.shape[0]):
+        for i in range(0, values.shape[1], LANES):
+            block = jnp.transpose(values[p * slots : (p + 1) * slots, i : i + LANES])
+            for k in range(LANES // head_dim):
+                head = (first + i) // head_dim + k
+                sums_ref[p, head : head + 1, :] = jnp.sum(
+                    block[k * head_dim : (k + 1) * head_dim], axis=0, keepdims=True
+                )
 
 
 def three_parts(values):
-    lane = lax.broadcasted_iota(jnp.int32, values.shape, 1)
     high = values.astype(bf16).astype(f32)
     rest = values - high
     middle = rest.astype(bf16).astype(f32)
-    low = rest - middle
-    parts = jnp.where(lane < HEADS, high, jnp.where(lane < 2 * HEADS, middle, low))
-    return parts.astype(bf16)
+    empty = jnp.zeros((LANES - 3 * HEADS, values.shape[1]), f32)
+    parts = jnp.concatenate([high, middle, rest - middle, empty], axis=0)
+    return jnp.transpose(parts).astype(bf16)
 
 
 def mix_kernel(
@@ -153,6 +151,9 @@
     key_grad,
     value_grad,
     leaving,
+    squares,
+    raw,
+    attn_grad,
 ):
     slots, recv_rows, _ = recv_ref.shape
     width = key_ref.shape[0]
@@ -172,48 +173,39 @@
 
     row = lax.broadcasted_iota(jnp.int32, (LANES, slots), 0)
     lookup = jnp.where(row == slot_ref[...], 1.0, 0.0).astype(bf16)
-    present = jnp.broadcast_to(presence_ref[...].astype(f32), (slots, LANES)).astype(bf16)
-    present = jnp.dot(present, lookup, preferred_element_type=f32)
-    valid = jnp.transpose(present) > 0.5
+    present = jnp.broadcast_to(presence_ref[...].astype(f32), (HEADS, LANES)).astype(bf16)
+    valid = jnp.dot(present, lookup, preferred_element_type=f32) > 0.5
 
     query = query_ref[...]
     grad = grad_ref[...].astype(f32)
-    selector = head_rows(width)
     spread = head_lanes(width)
-
-    squares = jnp.zeros((pairs * slots, LANES), f32)
-    raw = jnp.zeros((pairs * slots, LANES), f32)
-    attn_grad = jnp.zeros((pairs * slots, LANES), f32)
     for span in spans:
         block = jnp.dot(tokens[...], key_ref[:, span], preferred_element_type=f32)
         keys[:, span] = block
-        squares = squares + head_sums(block * block, selector[span])
-        raw = raw + head_sums(block * query[:, span], selector[span])
+        head_sums(block * block, squares, span.start, slots, head_dim)
+        head_sums(block * query[:, span], raw, span.start, slots, head_dim)
     for span in spans:
         block = jnp.dot(tokens[...], value_ref[:, span], preferred_element_type=f32)
         values[:, span] = block
-        product = jnp.concatenate([block[halves[p]] * grad[p : p + 1, span] for p in range(pairs)], axis=0)
-        attn_grad = attn_grad + head_sums(product, selector[span])
-
-    ratio = lax.rsqrt(squares * (1.0 / head_dim) + key_eps)
-    scores = raw * ratio * score_scale
-    attention, dscore = [], []
+        block = jnp.concatenate([block[halves[p]] * grad[p : p + 1, span] for p in range(pairs)], axis=0)
+        head_sums(block, attn_grad, span.start, slots, head_dim)
+
+    attention_parts, along_parts, across_parts = [], [], []
     for p in range(pairs):
-        part = scores[halves[p]]
-        top = jnp.max(jnp.where(valid, part, masked_low), axis=0, keepdims=True)
-        weights = jnp.where(valid, jnp.exp(part - top), 0.0)
-        weights = weights / jnp.sum(weights, axis=0, keepdims=True)
-        change = attn_grad[halves[p]]
-        inner = jnp.sum(weights * change, axis=0, keepdims=True)
-        attention.append(weights)
-        dscore.append(weights * (change - inner))
-    attention = jnp.concatenate(attention, axis=0)
-    dscore = jnp.concatenate(dscore, axis=0)
-    along = dscore * ratio * score_scale
-    across = dscore * scores * ratio * ratio * (1.0 / head_dim)
-    attention_parts = three_parts(attention)
-    along_parts = three_parts(along)
-    across_parts = three_parts(across)
+        ratio = lax.rsqrt(squares[p] * (1.0 / head_dim) + key_eps)
+        scores = raw[p] * ratio * score_scale
+        top = jnp.max(jnp.where(valid, scores, masked_low), axis=1, keepdims=True)
+        weights = jnp.where(valid, jnp.exp(scores - top), 0.0)
+        weights = weights / jnp.sum(weights, axis=1, keepdims=True)
+        change = attn_grad[p]
+        inner = jnp.sum(weights * change, axis=1, keepdims=True)
+        dscore = weights * (change - inner)
+        attention_parts.append(three_parts(weights))
+        along_parts.append(three_parts(dscore * ratio * score_scale))
+        across_parts.append(three_parts(dscore * scores * ratio * ratio * (1.0 / head_dim)))
+    attention_parts = jnp.concatenate(attention_parts, axis=0)
+    along_parts = jnp.concatenate(along_parts, axis=0)
+    across_parts = jnp.concatenate(across_parts, axis=0)
 
     for span in spans:
         weights = jnp.dot(attention_parts, spread[:, span], preferred_element_type=f32)
@@ -250,6 +242,21 @@
     send_ref[...] = leaving[...].reshape(send_ref.shape).astype(bf16)
 
 
+def mix_scratch(pairs, slots, width, rows, groups):
+    return [
+        pltpu.VMEM((slots * rows, LANES), f32),
+        pltpu.VMEM((pairs * slots, width), bf16),
+        pltpu.VMEM((pairs * slots, width), f32),
+        pltpu.VMEM((pairs * slots, width), f32),
+        pltpu.VMEM((pairs * slots, width), bf16),
+        pltpu.VMEM((pairs * slots, width), bf16),
+        pltpu.VMEM((slots * (rows + groups), LANES), f32),
+        pltpu.VMEM((pairs, HEADS, slots), f32),
+        pltpu.VMEM((pairs, HEADS, slots), f32),
+        pltpu.VMEM((pairs, HEADS, slots), f32),
+    ]
+
+
 def grad_kernel(recv_ref, normed_ref, out_ref, arrived, grads):
     owners, recv_rows, _ = recv_ref.shape
     width = grads.shape[1]
@@ -264,9 +271,7 @@
         for j in range(groups):
             block = arrived[pl.ds(p * groups + j, owners, stride=recv_rows), :]
             grads[p * owners : (p + 1) * owners, j * LANES : (j + 1) * LANES] = block.astype(bf16)
-    sums = lax.dot_general(
-        normed_ref[...], grads[...], (((0,), (0,)), ((), ())), preferred_element_type=f32
-    )
+    sums = jnp.dot(normed_ref[...], grads[...], preferred_element_type=f32)
     for j in range(groups):
         lanes = slice(j * LANES, (j + 1) * LANES)
         for c in range(copies):
@@ -289,7 +294,6 @@
         query_ref[:, lanes] = total[groups * (pixels + 1) + j : groups * (pixels + 1) + j + 1]
 
 
-smem = pl.BlockSpec(memory_space=pltpu.SMEM)
 vmem = pl.BlockSpec(memory_space=pltpu.VMEM)
 hbm = pl.BlockSpec(memory_space=pltpu.HBM)
 
@@ -320,26 +324,26 @@
 
     stats, fields, patch_weight, var_embed, present, slot_row, query_row, grad_rows = pl.pallas_call(
         stats_kernel,
-        out_shape=(jax.ShapeDtypeStruct((1, LANES), f32),)
+        out_shape=(pltpu.VMEM((1, LANES), f32),)
         + tuple(pltpu.VMEM(a.shape, a.dtype) for a in fixed),
-        in_specs=[smem, smem] + [hbm] * len(fixed),
+        in_specs=[hbm] * len(fixed),
         out_specs=[vmem] * (1 + len(fixed)),
         scratch_shapes=[pltpu.SemaphoreType.DMA((len(fixed),))],
         name="stats",
-    )(presence, slot_var, *fixed)
+    )(*fixed)
     stats = lax.all_gather(stats, "dp")
 
     tokens, normed = pl.pallas_call(
         token_kernel,
         out_shape=(
             jax.ShapeDtypeStruct((var_count, rows, LANES), bf16),
-            jax.ShapeDtypeStruct((patches, LANES), bf16),
+            jax.ShapeDtypeStruct((2 * pixels, patches), bf16),
         ),
         in_specs=[vmem] * 4,
         out_specs=(vmem, vmem),
-        scratch_shapes=[pltpu.VMEM((patches * groups, LANES), f32), pltpu.VMEM((patches, LANES), f32)],
+        scratch_shapes=[pltpu.VMEM((patches * groups, LANES), f32)],
         compiler_params=params(16),
-        cost_estimate=pl.CostEstimate(flops=FLOPS, bytes_accessed=BYTES, transcendentals=0),
+        cost_estimate=pl.CostEstimate(flops=6 * 10**9, bytes_accessed=2 * 10**6, transcendentals=0),
         name="tokens",
     )(stats, fields, patch_weight, var_embed)
     gathered = lax.all_to_all(tokens, "var", split_axis=0, concat_axis=0, tiled=True)
@@ -352,15 +356,7 @@
         ),
         in_specs=[vmem] * 7,
         out_specs=(vmem, vmem),
-        scratch_shapes=[
-            pltpu.VMEM((slots * rows, LANES), f32),
-            pltpu.VMEM((pairs * slots, width), bf16),
-            pltpu.VMEM((pairs * slots, width), f32),
-            pltpu.VMEM((pairs * slots, width), f32),
-            pltpu.VMEM((pairs * slots, width), bf16),
-            pltpu.VMEM((pairs * slots, width), bf16),
-            pltpu.VMEM((slots * (rows + groups), LANES), f32),
-        ],
+        scratch_shapes=mix_scratch(pairs, slots, width, rows, groups),
         compiler_params=params(32),
         name="mix",
     )(present, slot_row, gathered, key_weight, value_weight, query_row, grad_rows)
@@ -389,6 +385,7 @@
         ),
         in_specs=[vmem],
         out_specs=(vmem, vmem, vmem),
+        compiler_params=params(16),
         name="totals",
     )(parts)
     return (

time: 102 us -> 97.4 us (0.955)
  Pallas kernels: 10.9 us -> 7.14 us
    pallas_call x1, Pallas kernels: 5.9 us -> 4.25 us  [on_device(): pl.pallas_call(mix_kernel, out_shape=(jax.ShapeDtypeStruct((pairs, width)...]
    pallas_call x1, Pallas kernels: 2.13 us -> 1.07 us  [on_device(): pl.pallas_call(stats_kernel, out_shape=(pltpu.VMEM((1, LANES), f32),) + t...]
where the time goes in v3:
time: 97.4 us; the launch traced here: 97.1 us
  blocking collectives  89.3 us (92%)
  Pallas kernels  7.14 us (7%)
    all_to_all x1, blocking collectives, on_device(): lax.all_to_all(tokens, 'var', split_axis=0, concat_axis=0, tiled=True)  40.1 us
    all_to_all x1, blocking collectives, on_device(): lax.all_to_all(outgoing, 'var', split_axis=0, concat_axis=0, tiled=True)  31.1 us
    all_to_all x1, blocking collectives, on_device(): parts = lax.all_to_all(parts, 'dp', split_axis=0, concat_axis=0, tiled=True)  9.63 us
    all_gather x1, blocking collectives, on_device(): stats = lax.all_gather(stats, 'dp')  8.48 us
    pallas_call x1, Pallas kernels, on_device(): pl.pallas_call(mix_kernel, out_shape=(jax.ShapeDtypeStruct((pairs, width)...  4.25 us

profile of v3, /device:TPU:1, one launch (start us, length us, event | category | flops | bytes accessed | tf_op | source)
XLA Modules:
  0.0 97.1 jit_solution(3857016530556210847)
XLA Ops:
  0.6 1.1 %stats.1 = (f32[1,128]{1,0:T(1,128)S(1)}, bf16[16,256]{1,0:T(8,128)(2,1)S(1)}, bf16[16,1024]{1,0:T(8,128)(2,1)S(1)}, bf16[1,1024]{1,0:T(2,128)(2,1)S(1)}, s32[1,...) custom-call(bf16[16,256]{1,0:T(8,128)(2,1)} %bitcast.13, ...), custom_call_target="tpu_custom_call" | custom-call | tf_op jit(solution)/shard_map/stats/pallas_call | solution.py:325
  1.7 8.5 %all-gather.1.stats_ref = f32[4,1,128]{2,1,0:T(1,128)S(1)} all-gather(f32[1,1,128]{2,1,0:T(1,128)S(1)} %bitcast.11), channel_id=2, replica_groups=mesh['var'=128,'dp'=4] {'dp'}, dimensions={0}, use_global_device_ids=true | all-gather | bytes 2560 | tf_op jit(solution)/shard_map/all_gather | solution.py:334
  10.2 0.0 copy-start
  10.2 0.0 copy-start.1
  10.2 0.7 tokens.1
  10.9 40.1 %all_to_all.15.recv_ref = bf16[128,16,128]{2,1,0:T(8,128)(2,1)S(1)} all-to-all(bf16[128,16,128]{2,1,0:T(8,128)(2,1)S(1)} %get-tuple-element.25), channel_id=1, replica_groups=mesh['var'=128,'dp'=4] {'var'}, dimensions={0} | all-to-all | bytes 1048576 | tf_op jit(solution)/shard_map/all_to_all | solution.py:349
  51.0 0.0 copy-done
  51.0 0.0 copy-done.1
  51.0 4.3 %mix.1 = (bf16[2,1024]{1,0:T(2,128)(2,1)}, bf16[128,24,128]{2,1,0:T(8,128)(2,1)S(1)}) custom-call(s32[1,128]{1,0:T(1,128)S(1)} %get-tuple-element.19.presence_ref, s32[1,128]{1,0:T(1,128)S(1)} %get-tuple-element.20.slot_ref, bf16[128,16,128]{2,1,0:T(8,128)(2,1)S(1)} %all_to_all.15.recv_ref, bf16[1024,1024]{1,0:T(8,128)(2,1)S(1)} %copy-done, ...), custom_call_target="tpu_custom_call" | custom-call | tf_op jit(solution)/shard_map/mix/pallas_call | solution.py:351
  55.3 31.1 %all_to_all.16.recv_ref = bf16[128,24,128]{2,1,0:T(8,128)(2,1)S(1)} all-to-all(bf16[128,24,128]{2,1,0:T(8,128)(2,1)S(1)} %get-tuple-element.29), channel_id=1, replica_groups=mesh['var'=128,'dp'=4] {'var'}, dimensions={0} | all-to-all | bytes 1572864 | tf_op jit(solution)/shard_map/all_to_all | solution.py:363
  86.4 0.5 grads.1
  86.9 9.6 %all_to_all.17.parts_ref = f32[4,144,128]{2,1,0:T(8,128)S(1)} all-to-all(f32[4,144,128]{2,1,0:T(8,128)S(1)} %grads.1), channel_id=1, replica_groups=mesh['var'=128,'dp'=4] {'dp'}, dimensions={0} | all-to-all | bytes 589824 | tf_op jit(solution)/shard_map/all_to_all | solution.py:377
  96.5 0.7 totals.1
Async XLA Ops:
  10.2 40.8 %copy-start = (bf16[1024,1024]{1,0:T(8,128)(2,1)S(1)}, bf16[1024,1024]{1,0:T(8,128)(2,1)}, u32[]{:S(2)}) copy-start(bf16[1024,1024]{1,0:T(8,128)(2,1)} %key_ref.1) | copy-start | bytes 6291460
  10.2 40.8 %copy-start.1 = (bf16[1024,1024]{1,0:T(8,128)(2,1)S(1)}, bf16[1024,1024]{1,0:T(8,128)(2,1)}, u32[]{:S(2)}) copy-start(bf16[1024,1024]{1,0:T(8,128)(2,1)} %value_ref.1) | copy-start | bytes 6291460

commit v4 on v3

--- a/solution.py
+++ b/solution.py
@@ -257,7 +257,7 @@
     ]
 
 
-def grad_kernel(recv_ref, normed_ref, out_ref, arrived, grads):
+def grad_kernel(recv_ref, normed_ref, out_ref, arrived, grads, packed):
     owners, recv_rows, _ = recv_ref.shape
     width = grads.shape[1]
     groups = width // LANES
@@ -274,19 +274,19 @@
     sums = jnp.dot(normed_ref[...], grads[...], preferred_element_type=f32)
     for j in range(groups):
         lanes = slice(j * LANES, (j + 1) * LANES)
-        for c in range(copies):
-            out_ref[c, j * pixels : (j + 1) * pixels, :] = sums[:pixels, lanes]
-            out_ref[c, groups * pixels + j : groups * pixels + j + 1, :] = sums[
-                pixels : pixels + 1, lanes
-            ]
+        packed[j * pixels : (j + 1) * pixels, :] = sums[:pixels, lanes]
+        packed[groups * pixels + j : groups * pixels + j + 1, :] = sums[pixels : pixels + 1, lanes]
+    packed[groups * (pixels + 1) :, :] = dquery
+    total = packed[...].astype(bf16)
     for c in range(copies):
-        out_ref[c, groups * (pixels + 1) :, :] = dquery
+        out_ref[c] = total
 
 
 def total_kernel(parts_ref, weight_ref, embed_ref, query_ref):
     pixels, width = weight_ref.shape
     groups = width // LANES
-    total = (parts_ref[0] + parts_ref[1]) + (parts_ref[2] + parts_ref[3])
+    parts = [parts_ref[b].astype(f32) for b in range(parts_ref.shape[0])]
+    total = sum(parts[1:], parts[0])
     for j in range(groups):
         lanes = slice(j * LANES, (j + 1) * LANES)
         weight_ref[:, lanes] = total[j * pixels : (j + 1) * pixels]
@@ -364,12 +364,13 @@
 
     parts = pl.pallas_call(
         grad_kernel,
-        out_shape=jax.ShapeDtypeStruct((samples, groups * (pixels + 2), LANES), f32),
+        out_shape=jax.ShapeDtypeStruct((samples, groups * (pixels + 2), LANES), bf16),
         in_specs=[vmem, vmem],
         out_specs=vmem,
         scratch_shapes=[
             pltpu.VMEM((var_count * (rows + groups), LANES), f32),
             pltpu.VMEM((patches, width), bf16),
+            pltpu.VMEM((groups * (pixels + 2), LANES), f32),
         ],
         compiler_params=params(16),
         name="grads",

time: 97.4 us -> 95.8 us (0.984)
  blocking collectives: 89.3 us -> 87.7 us
    all_to_all x1, blocking collectives: 9.63 us -> 8.04 us  [on_device(): parts = lax.all_to_all(parts, 'dp', split_axis=0, concat_axis=0, tiled=True)]
where the time goes in v4:
time: 95.8 us; the launch traced here: 95.5 us
  blocking collectives  87.7 us (92%)
  Pallas kernels  7.14 us (7%)
    all_to_all x1, blocking collectives, on_device(): lax.all_to_all(tokens, 'var', split_axis=0, concat_axis=0, tiled=True)  40.1 us
    all_to_all x1, blocking collectives, on_device(): lax.all_to_all(outgoing, 'var', split_axis=0, concat_axis=0, tiled=True)  31.1 us
    all_gather x1, blocking collectives, on_device(): stats = lax.all_gather(stats, 'dp')  8.48 us
    all_to_all x1, blocking collectives, on_device(): parts = lax.all_to_all(parts, 'dp', split_axis=0, concat_axis=0, tiled=True)  8.04 us
    pallas_call x1, Pallas kernels, on_device(): pl.pallas_call(mix_kernel, out_shape=(jax.ShapeDtypeStruct((pairs, width)...  4.25 us

profile of v4, /device:TPU:1, one launch (start us, length us, event | category | flops | bytes accessed | tf_op | source)
XLA Modules:
  0.0 95.5 jit_solution(12326042695560390726)
XLA Ops:
  0.6 1.1 %stats.1 = (f32[1,128]{1,0:T(1,128)S(1)}, bf16[16,256]{1,0:T(8,128)(2,1)S(1)}, bf16[16,1024]{1,0:T(8,128)(2,1)S(1)}, bf16[1,1024]{1,0:T(2,128)(2,1)S(1)}, s32[1,...) custom-call(bf16[16,256]{1,0:T(8,128)(2,1)} %bitcast.13, ...), custom_call_target="tpu_custom_call" | custom-call | tf_op jit(solution)/shard_map/stats/pallas_call | solution.py:325
  1.7 8.5 %all-gather.1.stats_ref = f32[4,1,128]{2,1,0:T(1,128)S(1)} all-gather(f32[1,1,128]{2,1,0:T(1,128)S(1)} %bitcast.11), channel_id=2, replica_groups=mesh['var'=128,'dp'=4] {'dp'}, dimensions={0}, use_global_device_ids=true | all-gather | bytes 2560 | tf_op jit(solution)/shard_map/all_gather | solution.py:334
  10.2 0.0 copy-start
  10.2 0.0 copy-start.1
  10.2 0.7 tokens.1
  10.9 40.1 %all_to_all.15.recv_ref = bf16[128,16,128]{2,1,0:T(8,128)(2,1)S(1)} all-to-all(bf16[128,16,128]{2,1,0:T(8,128)(2,1)S(1)} %get-tuple-element.25), channel_id=1, replica_groups=mesh['var'=128,'dp'=4] {'var'}, dimensions={0} | all-to-all | bytes 1048576 | tf_op jit(solution)/shard_map/all_to_all | solution.py:349
  51.0 0.0 copy-done
  51.0 0.0 copy-done.1
  51.0 4.3 %mix.1 = (bf16[2,1024]{1,0:T(2,128)(2,1)}, bf16[128,24,128]{2,1,0:T(8,128)(2,1)S(1)}) custom-call(s32[1,128]{1,0:T(1,128)S(1)} %get-tuple-element.19.presence_ref, s32[1,128]{1,0:T(1,128)S(1)} %get-tuple-element.20.slot_ref, bf16[128,16,128]{2,1,0:T(8,128)(2,1)S(1)} %all_to_all.15.recv_ref, bf16[1024,1024]{1,0:T(8,128)(2,1)S(1)} %copy-done, ...), custom_call_target="tpu_custom_call" | custom-call | tf_op jit(solution)/shard_map/mix/pallas_call | solution.py:351
  55.3 31.1 %all_to_all.16.recv_ref = bf16[128,24,128]{2,1,0:T(8,128)(2,1)S(1)} all-to-all(bf16[128,24,128]{2,1,0:T(8,128)(2,1)S(1)} %get-tuple-element.29), channel_id=1, replica_groups=mesh['var'=128,'dp'=4] {'var'}, dimensions={0} | all-to-all | bytes 1572864 | tf_op jit(solution)/shard_map/all_to_all | solution.py:363
  86.4 0.5 grads.1
  86.8 8.0 %all_to_all.17.parts_ref = bf16[4,144,128]{2,1,0:T(8,128)(2,1)S(1)} all-to-all(bf16[4,144,128]{2,1,0:T(8,128)(2,1)S(1)} %grads.1), channel_id=1, replica_groups=mesh['var'=128,'dp'=4] {'dp'}, dimensions={0} | all-to-all | bytes 294912 | tf_op jit(solution)/shard_map/all_to_all | solution.py:378
  94.9 0.7 totals.1
Async XLA Ops:
  10.2 40.8 %copy-start = (bf16[1024,1024]{1,0:T(8,128)(2,1)S(1)}, bf16[1024,1024]{1,0:T(8,128)(2,1)}, u32[]{:S(2)}) copy-start(bf16[1024,1024]{1,0:T(8,128)(2,1)} %key_ref.1) | copy-start | bytes 6291460
  10.2 40.8 %copy-start.1 = (bf16[1024,1024]{1,0:T(8,128)(2,1)S(1)}, bf16[1024,1024]{1,0:T(8,128)(2,1)}, u32[]{:S(2)}) copy-start(bf16[1024,1024]{1,0:T(8,128)(2,1)} %value_ref.1) | copy-start | bytes 6291460

commit v5 on v4

--- a/solution.py
+++ b/solution.py
@@ -58,19 +58,19 @@
     for move in moves:
         move.start()
     lane = lax.broadcasted_iota(jnp.int32, stats_ref.shape, 1)
-    moves[0].wait()
-    moves[1].wait()
+    for move in moves[:3]:
+        move.wait()
     slot = jnp.where(lane == lax.axis_index("var"), slot_out[...], 0)
     slot = jnp.sum(slot.astype(f32), axis=1, keepdims=True).astype(jnp.int32)
     flag = jnp.where(lane == slot, presence_out[...], 0).astype(f32)
     flag = jnp.sum(flag, axis=1, keepdims=True)
-    moves[2].wait()
     values = fields_out[...].astype(f32)
     cells = values.shape[0] * values.shape[1]
     total = jnp.sum(jnp.sum(values, axis=0, keepdims=True), axis=1, keepdims=True)
     centered = values - total / cells
     squares = jnp.sum(jnp.sum(centered * centered, axis=0, keepdims=True), axis=1, keepdims=True)
-    stats_ref[...] = jnp.where(lane == 0, total, jnp.where(lane == 1, squares, 1.0)) * flag
+    stats = jnp.where(lane == 0, total, jnp.where(lane == 1, squares, 1.0))
+    stats_ref[...] = jnp.where(flag > 0.5, stats, 0.0)
     for move in moves[3:]:
         move.wait()
 

time: 95.8 us -> 95.7 us (level)
  no operation moved by 1% of the time
where the time goes in v5:
time: 95.7 us; the launch traced here: 95.5 us
  blocking collectives  87.8 us (92%)
  Pallas kernels  7.02 us (7%)
    all_to_all x1, blocking collectives, on_device(): lax.all_to_all(tokens, 'var', split_axis=0, concat_axis=0, tiled=True)  40.1 us
    all_to_all x1, blocking collectives, on_device(): lax.all_to_all(outgoing, 'var', split_axis=0, concat_axis=0, tiled=True)  31.1 us
    all_gather x1, blocking collectives, on_device(): stats = lax.all_gather(stats, 'dp')  8.48 us
    all_to_all x1, blocking collectives, on_device(): parts = lax.all_to_all(parts, 'dp', split_axis=0, concat_axis=0, tiled=True)  8.04 us
    pallas_call x1, Pallas kernels, on_device(): pl.pallas_call(mix_kernel, out_shape=(jax.ShapeDtypeStruct((pairs, width)...  4.23 us

profile of v5, /device:TPU:1, one launch (start us, length us, event | category | flops | bytes accessed | tf_op | source)
XLA Modules:
  0.0 95.5 jit_solution(16703769307137522393)
XLA Ops:
  0.6 1.0 %stats.1 = (f32[1,128]{1,0:T(1,128)S(1)}, bf16[16,256]{1,0:T(8,128)(2,1)S(1)}, bf16[16,1024]{1,0:T(8,128)(2,1)S(1)}, bf16[1,1024]{1,0:T(2,128)(2,1)S(1)}, s32[1,...) custom-call(bf16[16,256]{1,0:T(8,128)(2,1)} %bitcast.13, ...), custom_call_target="tpu_custom_call" | custom-call | tf_op jit(solution)/shard_map/stats/pallas_call | solution.py:325
  1.6 8.5 %all-gather.1.stats_ref = f32[4,1,128]{2,1,0:T(1,128)S(1)} all-gather(f32[1,1,128]{2,1,0:T(1,128)S(1)} %bitcast.11), channel_id=2, replica_groups=mesh['var'=128,'dp'=4] {'dp'}, dimensions={0}, use_global_device_ids=true | all-gather | bytes 2560 | tf_op jit(solution)/shard_map/all_gather | solution.py:334
  10.1 0.0 copy-start
  10.1 0.0 copy-start.1
  10.1 0.7 tokens.1
  10.8 40.1 %all_to_all.15.recv_ref = bf16[128,16,128]{2,1,0:T(8,128)(2,1)S(1)} all-to-all(bf16[128,16,128]{2,1,0:T(8,128)(2,1)S(1)} %get-tuple-element.25), channel_id=1, replica_groups=mesh['var'=128,'dp'=4] {'var'}, dimensions={0} | all-to-all | bytes 1048576 | tf_op jit(solution)/shard_map/all_to_all | solution.py:349
  50.9 0.0 copy-done
  50.9 0.0 copy-done.1
  50.9 4.2 %mix.1 = (bf16[2,1024]{1,0:T(2,128)(2,1)}, bf16[128,24,128]{2,1,0:T(8,128)(2,1)S(1)}) custom-call(s32[1,128]{1,0:T(1,128)S(1)} %get-tuple-element.19.presence_ref, s32[1,128]{1,0:T(1,128)S(1)} %get-tuple-element.20.slot_ref, bf16[128,16,128]{2,1,0:T(8,128)(2,1)S(1)} %all_to_all.15.recv_ref, bf16[1024,1024]{1,0:T(8,128)(2,1)S(1)} %copy-done, ...), custom_call_target="tpu_custom_call" | custom-call | tf_op jit(solution)/shard_map/mix/pallas_call | solution.py:351
  55.2 31.1 %all_to_all.16.recv_ref = bf16[128,24,128]{2,1,0:T(8,128)(2,1)S(1)} all-to-all(bf16[128,24,128]{2,1,0:T(8,128)(2,1)S(1)} %get-tuple-element.29), channel_id=1, replica_groups=mesh['var'=128,'dp'=4] {'var'}, dimensions={0} | all-to-all | bytes 1572864 | tf_op jit(solution)/shard_map/all_to_all | solution.py:363
  86.3 0.5 grads.1
  86.8 8.0 %all_to_all.17.parts_ref = bf16[4,144,128]{2,1,0:T(8,128)(2,1)S(1)} all-to-all(bf16[4,144,128]{2,1,0:T(8,128)(2,1)S(1)} %grads.1), channel_id=1, replica_groups=mesh['var'=128,'dp'=4] {'dp'}, dimensions={0} | all-to-all | bytes 294912 | tf_op jit(solution)/shard_map/all_to_all | solution.py:378
  94.8 0.7 totals.1
Async XLA Ops:
  10.1 40.8 %copy-start = (bf16[1024,1024]{1,0:T(8,128)(2,1)S(1)}, bf16[1024,1024]{1,0:T(8,128)(2,1)}, u32[]{:S(2)}) copy-start(bf16[1024,1024]{1,0:T(8,128)(2,1)} %key_ref.1) | copy-start | bytes 6291460
  10.1 40.8 %copy-start.1 = (bf16[1024,1024]{1,0:T(8,128)(2,1)S(1)}, bf16[1024,1024]{1,0:T(8,128)(2,1)}, u32[]{:S(2)}) copy-start(bf16[1024,1024]{1,0:T(8,128)(2,1)} %value_ref.1) | copy-start | bytes 6291460

commit v6 on v5

--- a/solution.py
+++ b/solution.py
@@ -9,6 +9,7 @@
 
 HEADS = 16
 LANES = 128
+TURNS = 4
 SPAN = 256
 
 field_eps = 1e-05
@@ -69,7 +70,8 @@
     total = jnp.sum(jnp.sum(values, axis=0, keepdims=True), axis=1, keepdims=True)
     centered = values - total / cells
     squares = jnp.sum(jnp.sum(centered * centered, axis=0, keepdims=True), axis=1, keepdims=True)
-    stats = jnp.where(lane == 0, total, jnp.where(lane == 1, squares, 1.0))
+    turn = lane % TURNS
+    stats = jnp.where(turn == 0, total, jnp.where(turn == 1, squares, 1.0))
     stats_ref[...] = jnp.where(flag > 0.5, stats, 0.0)
     for move in moves[3:]:
         move.wait()
@@ -80,15 +82,24 @@
     cells = float(patches * pixels)
     groups = weight_ref.shape[1] // LANES
     samples = stats_ref.shape[0]
-    sums = [stats_ref[b, :, 0:1] for b in range(samples)]
-    flags = [stats_ref[b, :, 2:3] for b in range(samples)]
+    lane = lax.broadcasted_iota(jnp.int32, (1, LANES), 1)
+    sums, squares, flags = [], [], []
+    for b in range(samples):
+        turned = [stats_ref[b]]
+        turned.extend(pltpu.roll(turned[0], k, 1) for k in range(1, TURNS))
+        for which, out in enumerate((sums, squares, flags)):
+            value = turned[0]
+            for k in range(1, TURNS):
+                value = jnp.where((lane + (TURNS - which)) % TURNS == k, turned[k], value)
+            out.append(value)
     cell_total = jnp.maximum(sum(flags[1:], flags[0]), 1.0) * cells
     mean = sum(sums[1:], sums[0]) / cell_total
     second = jnp.zeros_like(mean)
     for b in range(samples):
         shift = sums[b] / cells - mean
-        second = second + stats_ref[b, :, 1:2] + flags[b] * cells * shift * shift
+        second = second + squares[b] + flags[b] * cells * shift * shift
     scale = lax.rsqrt(second / cell_total + field_eps)
+    mean, scale = (jnp.concatenate([x] * (patches // LANES), axis=1) for x in (mean, scale))
     normed = ((fields_ref[...].astype(f32) - mean) * scale).astype(bf16)
     tokens = lax.dot_general(
         normed, weight_ref[...], (((0,), (0,)), ((), ())), preferred_element_type=f32

time: 95.7 us -> 95.5 us (level)
  no operation moved by 1% of the time
where the time goes in v6:
time: 95.5 us; the launch traced here: 95.2 us
  blocking collectives  87.7 us (92%)
  Pallas kernels  6.83 us (7%)
    all_to_all x1, blocking collectives, on_device(): lax.all_to_all(tokens, 'var', split_axis=0, concat_axis=0, tiled=True)  40.1 us
    all_to_all x1, blocking collectives, on_device(): lax.all_to_all(outgoing, 'var', split_axis=0, concat_axis=0, tiled=True)  31.1 us
    all_gather x1, blocking collectives, on_device(): stats = lax.all_gather(stats, 'dp')  8.48 us
    all_to_all x1, blocking collectives, on_device(): parts = lax.all_to_all(parts, 'dp', split_axis=0, concat_axis=0, tiled=True)  8.04 us
    pallas_call x1, Pallas kernels, on_device(): pl.pallas_call(mix_kernel, out_shape=(jax.ShapeDtypeStruct((pairs, width)...  4.23 us

profile of v6, /device:TPU:1, one launch (start us, length us, event | category | flops | bytes accessed | tf_op | source)
XLA Modules:
  0.0 95.2 jit_solution(2862480136341398347)
XLA Ops:
  0.6 1.0 %stats.1 = (f32[1,128]{1,0:T(1,128)S(1)}, bf16[16,256]{1,0:T(8,128)(2,1)S(1)}, bf16[16,1024]{1,0:T(8,128)(2,1)S(1)}, bf16[1,1024]{1,0:T(2,128)(2,1)S(1)}, s32[1,...) custom-call(bf16[16,256]{1,0:T(8,128)(2,1)} %bitcast.13, ...), custom_call_target="tpu_custom_call" | custom-call | tf_op jit(solution)/shard_map/stats/pallas_call | solution.py:336
  1.6 8.5 %all-gather.1.stats_ref = f32[4,1,128]{2,1,0:T(1,128)S(1)} all-gather(f32[1,1,128]{2,1,0:T(1,128)S(1)} %bitcast.11), channel_id=2, replica_groups=mesh['var'=128,'dp'=4] {'dp'}, dimensions={0}, use_global_device_ids=true | all-gather | bytes 2560 | tf_op jit(solution)/shard_map/all_gather | solution.py:345
  10.1 0.0 copy-start
  10.1 0.0 copy-start.1
  10.1 0.5 tokens.1
  10.6 40.1 %all_to_all.15.recv_ref = bf16[128,16,128]{2,1,0:T(8,128)(2,1)S(1)} all-to-all(bf16[128,16,128]{2,1,0:T(8,128)(2,1)S(1)} %get-tuple-element.25), channel_id=1, replica_groups=mesh['var'=128,'dp'=4] {'var'}, dimensions={0} | all-to-all | bytes 1048576 | tf_op jit(solution)/shard_map/all_to_all | solution.py:360
  50.7 0.0 copy-done
  50.7 0.0 copy-done.1
  50.7 4.2 %mix.1 = (bf16[2,1024]{1,0:T(2,128)(2,1)}, bf16[128,24,128]{2,1,0:T(8,128)(2,1)S(1)}) custom-call(s32[1,128]{1,0:T(1,128)S(1)} %get-tuple-element.19.presence_ref, s32[1,128]{1,0:T(1,128)S(1)} %get-tuple-element.20.slot_ref, bf16[128,16,128]{2,1,0:T(8,128)(2,1)S(1)} %all_to_all.15.recv_ref, bf16[1024,1024]{1,0:T(8,128)(2,1)S(1)} %copy-done, ...), custom_call_target="tpu_custom_call" | custom-call | tf_op jit(solution)/shard_map/mix/pallas_call | solution.py:362
  55.0 31.1 %all_to_all.16.recv_ref = bf16[128,24,128]{2,1,0:T(8,128)(2,1)S(1)} all-to-all(bf16[128,24,128]{2,1,0:T(8,128)(2,1)S(1)} %get-tuple-element.29), channel_id=1, replica_groups=mesh['var'=128,'dp'=4] {'var'}, dimensions={0} | all-to-all | bytes 1572864 | tf_op jit(solution)/shard_map/all_to_all | solution.py:374
  86.1 0.5 grads.1
  86.5 8.0 %all_to_all.17.parts_ref = bf16[4,144,128]{2,1,0:T(8,128)(2,1)S(1)} all-to-all(bf16[4,144,128]{2,1,0:T(8,128)(2,1)S(1)} %grads.1), channel_id=1, replica_groups=mesh['var'=128,'dp'=4] {'dp'}, dimensions={0} | all-to-all | bytes 294912 | tf_op jit(solution)/shard_map/all_to_all | solution.py:389
  94.6 0.7 totals.1
Async XLA Ops:
  10.1 40.6 %copy-start = (bf16[1024,1024]{1,0:T(8,128)(2,1)S(1)}, bf16[1024,1024]{1,0:T(8,128)(2,1)}, u32[]{:S(2)}) copy-start(bf16[1024,1024]{1,0:T(8,128)(2,1)} %key_ref.1) | copy-start | bytes 6291460
  10.1 40.6 %copy-start.1 = (bf16[1024,1024]{1,0:T(8,128)(2,1)S(1)}, bf16[1024,1024]{1,0:T(8,128)(2,1)}, u32[]{:S(2)}) copy-start(bf16[1024,1024]{1,0:T(8,128)(2,1)} %value_ref.1) | copy-start | bytes 6291460

commit v7 on v6

--- a/solution.py
+++ b/solution.py
@@ -10,7 +10,7 @@
 HEADS = 16
 LANES = 128
 TURNS = 4
-SPAN = 256
+SPAN = 1024
 
 field_eps = 1e-05
 key_eps = 1e-06
@@ -207,9 +207,11 @@
         scores = raw[p] * ratio * score_scale
         top = jnp.max(jnp.where(valid, scores, masked_low), axis=1, keepdims=True)
         weights = jnp.where(valid, jnp.exp(scores - top), 0.0)
-        weights = weights / jnp.sum(weights, axis=1, keepdims=True)
         change = attn_grad[p]
         inner = jnp.sum(weights * change, axis=1, keepdims=True)
+        share = 1.0 / jnp.sum(weights, axis=1, keepdims=True)
+        weights = weights * share
+        inner = inner * share
         dscore = weights * (change - inner)
         attention_parts.append(three_parts(weights))
         along_parts.append(three_parts(dscore * ratio * score_scale))

time: 95.5 us -> 95.4 us (level)
  no operation moved by 1% of the time
where the time goes in v7:
time: 95.4 us; the launch traced here: 95.2 us
  blocking collectives  87.8 us (92%)
  Pallas kernels  6.76 us (7%)
    all_to_all x1, blocking collectives, on_device(): lax.all_to_all(tokens, 'var', split_axis=0, concat_axis=0, tiled=True)  40.1 us
    all_to_all x1, blocking collectives, on_device(): lax.all_to_all(outgoing, 'var', split_axis=0, concat_axis=0, tiled=True)  31.1 us
    all_gather x1, blocking collectives, on_device(): stats = lax.all_gather(stats, 'dp')  8.48 us
    all_to_all x1, blocking collectives, on_device(): parts = lax.all_to_all(parts, 'dp', split_axis=0, concat_axis=0, tiled=True)  8.04 us
    pallas_call x1, Pallas kernels, on_device(): pl.pallas_call(mix_kernel, out_shape=(jax.ShapeDtypeStruct((pairs, width)...  4.16 us

profile of v7, /device:TPU:1, one launch (start us, length us, event | category | flops | bytes accessed | tf_op | source)
XLA Modules:
  0.0 95.2 jit_solution(6732954087324780021)
XLA Ops:
  0.6 1.0 %stats.1 = (f32[1,128]{1,0:T(1,128)S(1)}, bf16[16,256]{1,0:T(8,128)(2,1)S(1)}, bf16[16,1024]{1,0:T(8,128)(2,1)S(1)}, bf16[1,1024]{1,0:T(2,128)(2,1)S(1)}, s32[1,...) custom-call(bf16[16,256]{1,0:T(8,128)(2,1)} %bitcast.13, ...), custom_call_target="tpu_custom_call" | custom-call | tf_op jit(solution)/shard_map/stats/pallas_call | solution.py:338
  1.6 8.5 %all-gather.1.stats_ref = f32[4,1,128]{2,1,0:T(1,128)S(1)} all-gather(f32[1,1,128]{2,1,0:T(1,128)S(1)} %bitcast.11), channel_id=2, replica_groups=mesh['var'=128,'dp'=4] {'dp'}, dimensions={0}, use_global_device_ids=true | all-gather | bytes 2560 | tf_op jit(solution)/shard_map/all_gather | solution.py:347
  10.1 0.0 copy-start
  10.1 0.0 copy-start.1
  10.1 0.5 tokens.1
  10.6 40.1 %all_to_all.15.recv_ref = bf16[128,16,128]{2,1,0:T(8,128)(2,1)S(1)} all-to-all(bf16[128,16,128]{2,1,0:T(8,128)(2,1)S(1)} %get-tuple-element.25), channel_id=1, replica_groups=mesh['var'=128,'dp'=4] {'var'}, dimensions={0} | all-to-all | bytes 1048576 | tf_op jit(solution)/shard_map/all_to_all | solution.py:362
  50.7 0.0 copy-done
  50.7 0.0 copy-done.1
  50.7 4.2 %mix.1 = (bf16[2,1024]{1,0:T(2,128)(2,1)}, bf16[128,24,128]{2,1,0:T(8,128)(2,1)S(1)}) custom-call(s32[1,128]{1,0:T(1,128)S(1)} %get-tuple-element.19.presence_ref, s32[1,128]{1,0:T(1,128)S(1)} %get-tuple-element.20.slot_ref, bf16[128,16,128]{2,1,0:T(8,128)(2,1)S(1)} %all_to_all.15.recv_ref, bf16[1024,1024]{1,0:T(8,128)(2,1)S(1)} %copy-done, ...), custom_call_target="tpu_custom_call" | custom-call | tf_op jit(solution)/shard_map/mix/pallas_call | solution.py:364
  54.9 31.1 %all_to_all.16.recv_ref = bf16[128,24,128]{2,1,0:T(8,128)(2,1)S(1)} all-to-all(bf16[128,24,128]{2,1,0:T(8,128)(2,1)S(1)} %get-tuple-element.29), channel_id=1, replica_groups=mesh['var'=128,'dp'=4] {'var'}, dimensions={0} | all-to-all | bytes 1572864 | tf_op jit(solution)/shard_map/all_to_all | solution.py:376
  86.0 0.5 grads.1
  86.5 8.0 %all_to_all.17.parts_ref = bf16[4,144,128]{2,1,0:T(8,128)(2,1)S(1)} all-to-all(bf16[4,144,128]{2,1,0:T(8,128)(2,1)S(1)} %grads.1), channel_id=1, replica_groups=mesh['var'=128,'dp'=4] {'dp'}, dimensions={0} | all-to-all | bytes 294912 | tf_op jit(solution)/shard_map/all_to_all | solution.py:391
  94.5 0.7 totals.1
Async XLA Ops:
  10.1 40.6 %copy-start = (bf16[1024,1024]{1,0:T(8,128)(2,1)S(1)}, bf16[1024,1024]{1,0:T(8,128)(2,1)}, u32[]{:S(2)}) copy-start(bf16[1024,1024]{1,0:T(8,128)(2,1)} %key_ref.1) | copy-start | bytes 6291460
  10.1 40.6 %copy-start.1 = (bf16[1024,1024]{1,0:T(8,128)(2,1)S(1)}, bf16[1024,1024]{1,0:T(8,128)(2,1)}, u32[]{:S(2)}) copy-start(bf16[1024,1024]{1,0:T(8,128)(2,1)} %value_ref.1) | copy-start | bytes 6291460

commit v8 on v7

--- a/solution.py
+++ b/solution.py
@@ -67,9 +67,17 @@
     flag = jnp.sum(flag, axis=1, keepdims=True)
     values = fields_out[...].astype(f32)
     cells = values.shape[0] * values.shape[1]
-    total = jnp.sum(jnp.sum(values, axis=0, keepdims=True), axis=1, keepdims=True)
-    centered = values - total / cells
-    squares = jnp.sum(jnp.sum(centered * centered, axis=0, keepdims=True), axis=1, keepdims=True)
+    ones = jnp.ones((values.shape[1], LANES), bf16)
+    total = jnp.dot(fields_out[...], ones, preferred_element_type=f32)
+    total = jnp.sum(total, axis=0, keepdims=True)
+    mean = jnp.concatenate([total / cells] * (values.shape[1] // LANES), axis=1)
+    rest = (values - mean) * (values - mean)
+    squares = jnp.zeros((values.shape[0], LANES), f32)
+    for _ in range(3):
+        part = rest.astype(bf16)
+        squares = squares + jnp.dot(part, ones, preferred_element_type=f32)
+        rest = rest - part.astype(f32)
+    squares = jnp.sum(squares, axis=0, keepdims=True)
     turn = lane % TURNS
     stats = jnp.where(turn == 0, total, jnp.where(turn == 1, squares, 1.0))
     stats_ref[...] = jnp.where(flag > 0.5, stats, 0.0)

time: 95.4 us -> 95.6 us (level)
  no operation moved by 1% of the time
where the time goes in v8:
time: 95.6 us; the launch traced here: 95.3 us
  blocking collectives  87.8 us (92%)
  Pallas kernels  6.87 us (7%)
    all_to_all x1, blocking collectives, on_device(): lax.all_to_all(tokens, 'var', split_axis=0, concat_axis=0, tiled=True)  40.1 us
    all_to_all x1, blocking collectives, on_device(): lax.all_to_all(outgoing, 'var', split_axis=0, concat_axis=0, tiled=True)  31.1 us
    all_gather x1, blocking collectives, on_device(): stats = lax.all_gather(stats, 'dp')  8.48 us
    all_to_all x1, blocking collectives, on_device(): parts = lax.all_to_all(parts, 'dp', split_axis=0, concat_axis=0, tiled=True)  8.04 us
    pallas_call x1, Pallas kernels, on_device(): pl.pallas_call(mix_kernel, out_shape=(jax.ShapeDtypeStruct((pairs, width)...  4.16 us

profile of v8, /device:TPU:1, one launch (start us, length us, event | category | flops | bytes accessed | tf_op | source)
XLA Modules:
  0.0 95.3 jit_solution(9225952561211895471)
XLA Ops:
  0.6 1.1 %stats.1 = (f32[1,128]{1,0:T(1,128)S(1)}, bf16[16,256]{1,0:T(8,128)(2,1)S(1)}, bf16[16,1024]{1,0:T(8,128)(2,1)S(1)}, bf16[1,1024]{1,0:T(2,128)(2,1)S(1)}, s32[1,...) custom-call(bf16[16,256]{1,0:T(8,128)(2,1)} %bitcast.13, ...), custom_call_target="tpu_custom_call" | custom-call | tf_op jit(solution)/shard_map/stats/pallas_call | solution.py:346
  1.7 8.5 %all-gather.1.stats_ref = f32[4,1,128]{2,1,0:T(1,128)S(1)} all-gather(f32[1,1,128]{2,1,0:T(1,128)S(1)} %bitcast.11), channel_id=2, replica_groups=mesh['var'=128,'dp'=4] {'dp'}, dimensions={0}, use_global_device_ids=true | all-gather | bytes 2560 | tf_op jit(solution)/shard_map/all_gather | solution.py:355
  10.2 0.0 copy-start
  10.2 0.0 copy-start.1
  10.2 0.5 tokens.1
  10.7 40.1 %all_to_all.15.recv_ref = bf16[128,16,128]{2,1,0:T(8,128)(2,1)S(1)} all-to-all(bf16[128,16,128]{2,1,0:T(8,128)(2,1)S(1)} %get-tuple-element.25), channel_id=1, replica_groups=mesh['var'=128,'dp'=4] {'var'}, dimensions={0} | all-to-all | bytes 1048576 | tf_op jit(solution)/shard_map/all_to_all | solution.py:370
  50.9 0.0 copy-done
  50.9 0.0 copy-done.1
  50.9 4.2 %mix.1 = (bf16[2,1024]{1,0:T(2,128)(2,1)}, bf16[128,24,128]{2,1,0:T(8,128)(2,1)S(1)}) custom-call(s32[1,128]{1,0:T(1,128)S(1)} %get-tuple-element.19.presence_ref, s32[1,128]{1,0:T(1,128)S(1)} %get-tuple-element.20.slot_ref, bf16[128,16,128]{2,1,0:T(8,128)(2,1)S(1)} %all_to_all.15.recv_ref, bf16[1024,1024]{1,0:T(8,128)(2,1)S(1)} %copy-done, ...), custom_call_target="tpu_custom_call" | custom-call | tf_op jit(solution)/shard_map/mix/pallas_call | solution.py:372
  55.0 31.1 %all_to_all.16.recv_ref = bf16[128,24,128]{2,1,0:T(8,128)(2,1)S(1)} all-to-all(bf16[128,24,128]{2,1,0:T(8,128)(2,1)S(1)} %get-tuple-element.29), channel_id=1, replica_groups=mesh['var'=128,'dp'=4] {'var'}, dimensions={0} | all-to-all | bytes 1572864 | tf_op jit(solution)/shard_map/all_to_all | solution.py:384
  86.1 0.5 grads.1
  86.6 8.0 %all_to_all.17.parts_ref = bf16[4,144,128]{2,1,0:T(8,128)(2,1)S(1)} all-to-all(bf16[4,144,128]{2,1,0:T(8,128)(2,1)S(1)} %grads.1), channel_id=1, replica_groups=mesh['var'=128,'dp'=4] {'dp'}, dimensions={0} | all-to-all | bytes 294912 | tf_op jit(solution)/shard_map/all_to_all | solution.py:399
  94.6 0.7 totals.1
Async XLA Ops:
  10.2 40.6 %copy-start = (bf16[1024,1024]{1,0:T(8,128)(2,1)S(1)}, bf16[1024,1024]{1,0:T(8,128)(2,1)}, u32[]{:S(2)}) copy-start(bf16[1024,1024]{1,0:T(8,128)(2,1)} %key_ref.1) | copy-start | bytes 6291460
  10.2 40.6 %copy-start.1 = (bf16[1024,1024]{1,0:T(8,128)(2,1)S(1)}, bf16[1024,1024]{1,0:T(8,128)(2,1)}, u32[]{:S(2)}) copy-start(bf16[1024,1024]{1,0:T(8,128)(2,1)} %value_ref.1) | copy-start | bytes 6291460
